TPU v7x, 512 devices: a whole 4x4x16 slice. The times are simulated.
512 devices in a mesh: dp: 32 (over z, core), tensor: 16 (over y, x).
Axes of the slice: x: 4, y: 4, z: 16, core: 2. Of those that a mesh axis runs over, the one named last changes fastest.
Arguments:
- attn_out: bfloat16 [8192, 8192], P('dp', 'tensor'), parts along dimension 0, may hold values from -6 to 6
- head_signs: int32 [64], replicated, may hold values from 0 to 1
- w_out: bfloat16 [8192, 8192], P('tensor'), may hold values from -0.09375 to 0.09375
- out_exp: int32 [8192], P('tensor'), may hold values from -2 to 1
- residual: bfloat16 [8192, 8192], P('dp', 'tensor'), parts along dimension 0, may hold values from -60 to 60
- norm_gain: bfloat16 [8192], P('tensor'), may hold values from 0.25 to 1.75
- w_kv: bfloat16 [8192, 2048], P(None, 'tensor'), may hold values from -0.0625 to 0.0625
- kv_exp: int32 [2048], P('tensor'), may hold values from -2 to 1
Outputs:
- resid_out: bfloat16 [8192, 8192], P('dp', 'tensor'), parts along dimension 0
- kv: bfloat16 [8192, 2048], P('dp', 'tensor'), parts along dimension 0
There are 32 independent parts, one for each index of `dp`. A program takes and returns all parts, laid end to end along the dimension named above; an argument that names none is the same for every part. Nothing has to cross between parts.
Inputs may be any that keep to these rules, and one draw needn't show every extreme that they name: The sign of head h is 2 head_signs[h] - 1.
All inputs are finite; a program needn't handle non-finite values.
Results may differ from a plain program's by a relative error of at most 0.025.
Values may be sent and summed in bfloat16 or wider, within the bound.
A program may use at most 64 MiB of HBM per device.

v0:
```python
import jax
import jax.numpy as jnp
from jax import lax
from jax.sharding import PartitionSpec as P

HD = 128
D = 8192


def from_partner(block, axis, stride):
    count = lax.axis_size(axis)
    route = []
    for low in range(count):
        high = low | 1 << stride
        if high != low and high < count:
            route += [(low, high), (high, low)]
    return lax.ppermute(block, axis, route)


def sylvester(order):
    row_ids = jnp.arange(order, dtype=jnp.int32)
    parity = jnp.zeros((order, order), jnp.int32)
    for bit_level in range(order.bit_length() - 1):
        parity = parity ^ row_ids[:, None] >> bit_level & row_ids[None, :] >> bit_level & 1
    return (1 - 2 * parity).astype(jnp.float32)


def body(attn_out, head_signs, w_out, out_exp, residual, norm_gain, w_kv, kv_exp):
    groups = lax.axis_size("tensor")
    my_index = lax.axis_index("tensor")
    tok_rows = attn_out.shape[0]
    local_heads = attn_out.shape[1] // HD
    head_total = local_heads * groups
    sign_values = (2 * head_signs - 1).astype(jnp.float32)
    my_signs = lax.dynamic_slice_in_dim(sign_values, my_index * local_heads, local_heads)
    signed = (
        attn_out.reshape(tok_rows, local_heads, HD).astype(jnp.float32) * my_signs[None, :, None]
    )
    blended = jnp.einsum(
        "thd,hg->tgd", signed, sylvester(local_heads), precision=lax.Precision.HIGHEST
    )
    for bit_level in range(groups.bit_length() - 1):
        partner = from_partner(blended.astype(jnp.bfloat16), "tensor", bit_level).astype(
            blended.dtype
        )
        is_upper = my_index >> bit_level & 1 == 1
        blended = jnp.where(is_upper, partner - blended, blended + partner)
    rotated = (
        (blended * head_total ** (-0.5)).astype(jnp.bfloat16).reshape(tok_rows, local_heads * HD)
    )
    summed = lax.psum_scatter(
        lax.dot_general(
            w_out, rotated, (((0,), (1,)), ((), ())), preferred_element_type=jnp.float32
        ).astype(jnp.bfloat16),
        "tensor",
        scatter_dimension=0,
        tiled=True,
    ).astype(jnp.float32)
    projected = summed.T * jnp.exp2(out_exp.astype(jnp.float32))[None, :]
    resid_out = (residual.astype(jnp.float32) + projected).astype(jnp.bfloat16)
    hidden_f = resid_out.astype(jnp.float32)
    partial_sq = jnp.sum(hidden_f * hidden_f, axis=1)
    total_sq = lax.psum(partial_sq, "tensor")
    inv_rms = lax.rsqrt(total_sq / D + 1e-05)
    normed = (hidden_f * inv_rms[:, None] * norm_gain.astype(jnp.float32)[None, :]).astype(
        jnp.bfloat16
    )
    kv_acc = jnp.dot(
        lax.all_gather(normed, "tensor", axis=1, tiled=True),
        w_kv,
        preferred_element_type=jnp.float32,
    )
    kv = (kv_acc * jnp.exp2(kv_exp.astype(jnp.float32))[None, :]).astype(jnp.bfloat16)
    return (resid_out, kv)


def solution(mesh):
    placed = (
        P("dp", "tensor"),
        P(),
        P("tensor", None),
        P("tensor"),
        P("dp", "tensor"),
        P("tensor"),
        P(None, "tensor"),
        P("tensor"),
    )
    return jax.shard_map(
        body,
        mesh=mesh,
        in_specs=placed,
        out_specs=(P("dp", "tensor"), P("dp", "tensor")),
        check_vma=False,
    )
```

profile of v0, /device:TPU:6, one launch (start us, length us, event | category | flops | bytes accessed | tf_op | source)
XLA Modules:
  0.0 278.3 jit_solution(14771514907342466310)
XLA Ops:
  7.2 0.8 add_convert_fusion
  8.0 1.1 reshape.36
  9.2 0.1 dynamic_slice.3
  9.2 1.8 fusion.38
  11.0 2.7 collective-permute-start
  13.7 7.4 %collective-permute-done = bf16[256,4,128]{2,1,0:T(4,128)(2,1)S(1)} collective-permute-done((bf16[256,4,128]{2,1,0:T(4,128)(2,1)}, bf16[256,4,128]{2,1,0:T(4,128)(2,1)S(1)}, u32[]{:S(2)}, u32[]{:S(2)}) %collective-permute-start) | collective-permute-done | bytes 262176 | tf_op jit(solution)/shard_map/ppermute | solution.py:17
  21.1 0.2 fusion.17
  21.3 5.5 %collective-permute-start.1 = (bf16[256,4,128]{2,1,0:T(4,128)(2,1)S(1)}, bf16[256,4,128]{2,1,0:T(4,128)(2,1)}, u32[]{:S(2)}, u32[]{:S(2)}) collective-permute-start(bf16[256,4,128]{2,1,0:T(4,128)(2,1)S(1)} %fusion.17), channel_id=1, source_target_pairs={{0,2},{2,0},{1,3},{3,1},{4,6},{6,4},{5,7},{7,5},{8,10},{10,8},{9,1... | collective-permute-start | bytes 786440 | tf_op jit(solution)/shard_map/ppermute | solution.py:17
  26.9 5.1 %collective-permute-done.1 = bf16[256,4,128]{2,1,0:T(4,128)(2,1)} collective-permute-done((bf16[256,4,128]{2,1,0:T(4,128)(2,1)S(1)}, bf16[256,4,128]{2,1,0:T(4,128)(2,1)}, u32[]{:S(2)}, u32[]{:S(2)}) %collective-permute-start.1) | collective-permute-done | bytes 262176 | tf_op jit(solution)/shard_map/ppermute | solution.py:17
  32.0 2.0 fusion.36
  34.0 3.5 %collective-permute-start.2 = (bf16[256,4,128]{2,1,0:T(4,128)(2,1)}, bf16[256,4,128]{2,1,0:T(4,128)(2,1)S(1)}, u32[]{:S(2)}, u32[]{:S(2)}) collective-permute-start(bf16[256,4,128]{2,1,0:T(4,128)(2,1)} %get-tuple-element.4), channel_id=1, source_target_pairs={{0,4},{4,0},{1,5},{5,1},{2,6},{6,2},{3,7},{7,3},{8,12},{12,8},{9,1... | collective-permute-start | bytes 786440 | tf_op jit(solution)/shard_map/ppermute | solution.py:17
  37.4 5.0 %collective-permute-done.2 = bf16[256,4,128]{2,1,0:T(4,128)(2,1)S(1)} collective-permute-done((bf16[256,4,128]{2,1,0:T(4,128)(2,1)}, bf16[256,4,128]{2,1,0:T(4,128)(2,1)S(1)}, u32[]{:S(2)}, u32[]{:S(2)}) %collective-permute-start.2) | collective-permute-done | bytes 262176 | tf_op jit(solution)/shard_map/ppermute | solution.py:17
  42.4 0.2 fusion.16
  42.6 5.1 %collective-permute-start.3 = (bf16[256,4,128]{2,1,0:T(4,128)(2,1)S(1)}, bf16[256,4,128]{2,1,0:T(4,128)(2,1)S(1)}, u32[]{:S(2)}, u32[]{:S(2)}) collective-permute-start(bf16[256,4,128]{2,1,0:T(4,128)(2,1)S(1)} %fusion.16), channel_id=1, source_target_pairs={{0,8},{8,0},{1,9},{9,1},{2,10},{10,2},{3,11},{11,3},{4,12},{12,4},... | collective-permute-start | bytes 786440 | tf_op jit(solution)/shard_map/ppermute | solution.py:17
  47.7 4.7 %collective-permute-done.3 = bf16[256,4,128]{2,1,0:T(4,128)(2,1)S(1)} collective-permute-done((bf16[256,4,128]{2,1,0:T(4,128)(2,1)S(1)}, bf16[256,4,128]{2,1,0:T(4,128)(2,1)S(1)}, u32[]{:S(2)}, u32[]{:S(2)}) %collective-permute-start.3) | collective-permute-done | bytes 262176 | tf_op jit(solution)/shard_map/ppermute | solution.py:17
  52.4 0.3 fusion.7
  52.7 7.7 %fusion = bf16[8192,256]{0,1:T(8,128)(2,1)} fusion(bf16[512,8192]{1,0:T(8,128)(2,1)} %param.10, bf16[32,8,4,128]{3,2,1,0:T(4,128)(2,1)S(1)} %bitcast.21), kind=kOutput, calls=%fused_computation.1 | convolution fusion | flops 2149580800 | bytes 12845056 | tf_op jit(solution)/shard_map/dot_general | solution.py:52
  60.5 0.6 copy-done.4
  61.1 96.5 %reduce-scatter.2.cloned.1.call-done = bf16[512,256]{0,1:T(8,128)(2,1)} async-done(((bf16[8192,256]{0,1:T(8,128)(2,1)}), bf16[512,256]{0,1:T(8,128)(2,1)}) %reduce-scatter.2.cloned.1.call-update) | async-done | bytes 262160 | tf_op jit(solution)/shard_map/reduce_scatter | solution.py:51
  157.6 1.1 fusion.8
  158.8 32.4 %psum.7 = f32[256]{0:T(256)S(1)} all-reduce(f32[256]{0:T(256)S(1)} %get-tuple-element.2), channel_id=1, replica_groups=mesh['dp'=32,'tensor'=16] {'tensor'}, use_global_device_ids=true, to_apply=%region_2.3 | all-reduce | flops 256 | bytes 2048 | tf_op jit(solution)/shard_map/psum | solution.py:63
  191.2 0.8 fusion.10
  192.1 75.3 %all-gather.2.cloned.1.call-done = bf16[256,8192]{1,0:T(8,128)(2,1)} async-done(((bf16[256,512]{1,0:T(8,128)(2,1)}), bf16[256,8192]{1,0:T(8,128)(2,1)}) %all-gather.2.cloned.1.call-update) | async-done | bytes 4194320 | tf_op jit(solution)/shard_map/all_gather | solution.py:69
  267.4 4.1 %fusion.1 = bf16[256,128]{1,0:T(8,128)(2,1)} fusion(bf16[256,8192]{1,0:T(8,128)(2,1)} %all-gather.2.cloned.1.call-done, bf16[8192,128]{1,0:T(8,128)(2,1)S(1)} %copy-done, f32[128]{0:T(128)S(1)} %multiply_exponential_fusion.1), kind=kOutput, calls=%fused_computation.4 | convolution fusion | flops 536936448 | bytes 6357504 | tf_op jit(solution)/shard_map/dot_general | solution.py:68
  (20 shorter events, 0.2 us)
Async XLA Ops:
  7.2 260.2 %copy-start = (bf16[8192,128]{1,0:T(8,128)(2,1)S(1)}, bf16[8192,128]{1,0:T(8,128)(2,1)}, u32[]{:S(2)}) copy-start(bf16[8192,128]{1,0:T(8,128)(2,1)} %param.14) | copy-start | bytes 6291460
  7.2 150.5 %reduce-scatter.2.cloned.1.call-start = ((), (), s32[]{:S(2)}) async-start(), calls=%async_computation.1 | async-start | bytes 4456448 | tf_op jit(solution)/shard_map/reduce_scatter | solution.py:51
  11.0 10.1 %collective-permute-start = (bf16[256,4,128]{2,1,0:T(4,128)(2,1)}, bf16[256,4,128]{2,1,0:T(4,128)(2,1)S(1)}, u32[]{:S(2)}, u32[]{:S(2)}) collective-permute-start(bf16[256,4,128]{2,1,0:T(4,128)(2,1)} %get-tuple-element.6), channel_id=1, source_target_pairs={{0,1},{1,0},{2,3},{3,2},{4,5},{5,4},{6,7},{7,6},{8,9},{9,8},{10,11... | collective-permute-start | bytes 786440 | tf_op jit(solution)/shard_map/ppermute | solution.py:17
  21.3 10.7 %collective-permute-start.1 = (bf16[256,4,128]{2,1,0:T(4,128)(2,1)S(1)}, bf16[256,4,128]{2,1,0:T(4,128)(2,1)}, u32[]{:S(2)}, u32[]{:S(2)}) collective-permute-start(bf16[256,4,128]{2,1,0:T(4,128)(2,1)S(1)} %fusion.17), channel_id=1, source_target_pairs={{0,2},{2,0},{1,3},{3,1},{4,6},{6,4},{5,7},{7,5},{8,10},{10,8},{9,1... | collective-permute-start | bytes 786440 | tf_op jit(solution)/shard_map/ppermute | solution.py:17
  34.0 8.5 %collective-permute-start.2 = (bf16[256,4,128]{2,1,0:T(4,128)(2,1)}, bf16[256,4,128]{2,1,0:T(4,128)(2,1)S(1)}, u32[]{:S(2)}, u32[]{:S(2)}) collective-permute-start(bf16[256,4,128]{2,1,0:T(4,128)(2,1)} %get-tuple-element.4), channel_id=1, source_target_pairs={{0,4},{4,0},{1,5},{5,1},{2,6},{6,2},{3,7},{7,3},{8,12},{12,8},{9,1... | collective-permute-start | bytes 786440 | tf_op jit(solution)/shard_map/ppermute | solution.py:17
  42.6 9.8 %collective-permute-start.3 = (bf16[256,4,128]{2,1,0:T(4,128)(2,1)S(1)}, bf16[256,4,128]{2,1,0:T(4,128)(2,1)S(1)}, u32[]{:S(2)}, u32[]{:S(2)}) collective-permute-start(bf16[256,4,128]{2,1,0:T(4,128)(2,1)S(1)} %fusion.16), channel_id=1, source_target_pairs={{0,8},{8,0},{1,9},{9,1},{2,10},{10,2},{3,11},{11,3},{4,12},{12,4},... | collective-permute-start | bytes 786440 | tf_op jit(solution)/shard_map/ppermute | solution.py:17
  60.4 0.7 copy-start.4
  60.4 0.7 copy-start.3
  60.4 97.2 %copy-start.2 = (bf16[256,512]{1,0:T(8,128)(2,1)S(1)}, bf16[256,512]{1,0:T(8,128)(2,1)}, u32[]{:S(2)}) copy-start(bf16[256,512]{1,0:T(8,128)(2,1)} %param.12) | copy-start | bytes 786436
  60.4 131.7 %copy-start.5 = (s32[128]{0:T(128)S(1)}, s32[128]{0:T(128)}, u32[]{:S(2)}) copy-start(s32[128]{0:T(128)} %param.15) | copy-start | bytes 1540
  60.4 206.9 %all-gather.2.cloned.1.call-start = ((), (), s32[]{:S(2)}) async-start(), calls=%async_computation.2 | async-start | bytes 4456448 | tf_op jit(solution)/shard_map/all_gather | solution.py:69
  158.8 112.6 %copy-start.1 = (bf16[256,512]{1,0:T(8,128)(2,1)}, bf16[256,512]{1,0:T(8,128)(2,1)S(1)}, u32[]{:S(2)}) copy-start(bf16[256,512]{1,0:T(8,128)(2,1)S(1)} %get-tuple-element.3) | copy-start | bytes 786436
Sparse Core Ops, SparseCore 0:
  60.6 97.0 reduce-scatter.1
  192.2 75.1 all-gather.1
where the time goes:
time: 279 us; the launch traced here: 278 us
  waiting for transfers between devices  194 us (70%)
  blocking collectives  32.4 us (12%)
  starting transfers between devices  16.9 us (6%)
  between operations  14.2 us (5%)
  matrix products  13.5 us (5%)
  other arithmetic  5.46 us (2%)
    reduce_scatter x1, waiting for transfers between devices, body(): lax.psum_scatter(lax.dot_general(w_out, rotated, (((0,), (1,)), ((), ()))...  96.5 us
    all_gather x1, waiting for transfers between devices, body(): lax.all_gather(normed, 'tensor', axis=1, tiled=True)  75.3 us
    psum x1, blocking collectives, body(): total_sq = lax.psum(partial_sq, 'tensor')  32.4 us
    ppermute x4, waiting for transfers between devices, from_partner(): return lax.ppermute(block, axis, route)  22.2 us
    ppermute x4, starting transfers between devices, from_partner(): return lax.ppermute(block, axis, route)  16.8 us
    dot_general x1, matrix products, body(): lax.dot_general(w_out, rotated, (((0,), (1,)), ((), ())), preferred_eleme...  7.7 us
  transfers between devices with their start and end apart: 6, of which 6 were waited for; matrix products, arithmetic and copies ran while one was open for 0% of the time, Pallas kernels for 0%

commit v1 on v0

v1 whole, which is shorter than its diff:
```python
import functools

import jax
import jax.numpy as jnp
from jax import lax
from jax.experimental import pallas as pl
from jax.experimental.pallas import tpu as pltpu
from jax.sharding import PartitionSpec as P

MESH = pl.DeviceIdType.MESH
BF16 = jnp.bfloat16
F32 = jnp.float32
HD = 128
LH = 4
N = 16
TOK = 256
BLK = 512
D = N * BLK
KVB = 128
GROUPS = 2
GR = TOK // GROUPS
HR = GR // 2
QR = HR // 2
CHUNKS = (2, 1, 3, 0)
ORDER = (
    (2, 2), (1, 2), (2, 1), (3, 2), (2, 3), (0, 2), (2, 0), (1, 1),
    (1, 3), (3, 1), (3, 3), (0, 1), (0, 3), (1, 0), (3, 0), (0, 0),
)


def hadamard(vals):
    step = 1
    while step < len(vals):
        out = list(vals)
        for i in range(len(vals)):
            if not i & step:
                out[i] = vals[i] + vals[i | step]
                out[i | step] = vals[i] - vals[i | step]
        vals = out
        step *= 2
    return vals


def kernel(
    n_dp,
    attn, signs, w_out, out_exp, residual, gain, w_kv, kv_exp,
    resid_out, kv_out,
    sgn, att, mixed, turned, rot, w, pb, s1, f, q, own, s1b, fb,
    wkv, xn, kp, kr, sqs, sqr, res, ro, gn, oe, ke, ko,
    in_sem, w_sem, out_sem,
    a_send, a_recv, k_send, k_recv, r_send, r_recv,
    p_send, s1_recv, f_recv, q_send, s1b_recv, fb_recv,
    z_send, zr_recv, zl_recv, sib_recv,
    kv_send, kv_recv, sq_send, sq_recv,
):
    me = lax.axis_index("tensor")
    dp = lax.axis_index("dp")
    y, x = me // 4, lax.rem(me, 4)
    z, core = dp // 2, lax.rem(dp, 2)
    nz = n_dp // 2
    ck = BLK // n_dp

    def at_yx(dy, dx):
        return lax.rem(y + dy, 4) * 4 + lax.rem(x + dx, 4)

    along = (
        ({"tensor": at_yx(0, 1)}, {"tensor": at_yx(0, 3)}),
        ({"tensor": at_yx(1, 0)}, {"tensor": at_yx(3, 0)}),
    )
    z_up = {"dp": lax.rem(z + 1, nz) * 2 + core}
    z_down = {"dp": lax.rem(z + nz - 1, nz) * 2 + core}
    sibling = {"dp": z * 2 + 1 - core}

    def send(src, dst, send_sem, recv_sem, to):
        pltpu.make_async_remote_copy(
            src_ref=src, dst_ref=dst, send_sem=send_sem, recv_sem=recv_sem,
            device_id=to, device_id_type=MESH,
        ).start()

    def wait(ref, sem):
        pltpu.make_async_copy(ref, ref, sem).wait()

    def to_peers(fn):
        def one(k, carry):
            fn(lax.rem(me + k, N))
            return carry

        lax.fori_loop(1, N, one, 0)

    mine = pl.ds(pl.multiple_of(me * 16, 16), 16)
    my_rows = pl.ds(pl.multiple_of(dp * ck, ck), ck)
    my_cols = pl.ds(pl.multiple_of(me * KVB, KVB), KVB)
    loads = [
        pltpu.make_async_copy(attn.at[mine, :], att.at[me], in_sem.at[0]),
        pltpu.make_async_copy(signs, sgn, in_sem.at[1]),
        pltpu.make_async_copy(
            w_kv.at[pl.ds(pl.multiple_of(me * BLK + dp * ck, ck), ck), :],
            wkv.at[my_rows, my_cols], in_sem.at[2],
        ),
        pltpu.make_async_copy(out_exp, oe, in_sem.at[3]),
        pltpu.make_async_copy(residual, res, in_sem.at[4]),
        pltpu.make_async_copy(gain, gn, in_sem.at[5]),
        pltpu.make_async_copy(kv_exp, ke, in_sem.at[6]),
    ]
    for copy in loads:
        copy.start()

    w_loads = {}
    for i, (dy, dx) in enumerate(ORDER):
        columns = pl.ds(pl.multiple_of(at_yx(dy, dx) * BLK, BLK), BLK)
        w_loads[dy, dx] = pltpu.make_async_copy(w_out.at[:, columns], w.at[dy, dx], w_sem.at[i])

    barrier = pltpu.get_barrier_semaphore()

    def greet(j):
        pl.semaphore_signal(barrier, inc=1, device_id={"tensor": j}, device_id_type=MESH)

    to_peers(greet)
    for to in (z_up, z_down, sibling):
        pl.semaphore_signal(barrier, inc=1, device_id=to, device_id_type=MESH)
    pl.semaphore_wait(barrier, N - 1 + 3)

    def send_tokens(j):
        rows = pl.ds(pl.multiple_of(j * 16, 16), 16)
        send(attn.at[rows, :], att.at[me], a_send, a_recv, {"tensor": j})

    to_peers(send_tokens)

    def send_kv_rows(j):
        rows = pl.ds(pl.multiple_of(j * BLK + dp * ck, ck), ck)
        send(w_kv.at[rows, :], wkv.at[my_rows, my_cols], k_send, k_recv, {"tensor": j})

    to_peers(send_kv_rows)
    for dy, dx in ORDER:
        w_loads[dy, dx].start()

    loads[0].wait()
    loads[1].wait()
    wait(att.at[pl.ds(0, N - 1)], a_recv)
    for s in range(N):
        heads = []
        for h in range(LH):
            sign = (2 * sgn[s * LH + h] - 1).astype(F32)
            heads.append(att[s, :, h * HD : (h + 1) * HD].astype(F32) * sign)
        for h, val in enumerate(hadamard(heads)):
            mixed[s, :, h * HD : (h + 1) * HD] = val
    for h in range(LH):
        at = slice(h * HD, (h + 1) * HD)
        for g, val in enumerate(hadamard([mixed[s, :, at] for s in range(N)])):
            turned[g, :, at] = (val * 0.125).astype(BF16)

    def send_turned(j):
        send(turned.at[j], rot.at[mine, :], r_send, r_recv, {"tensor": j})

    to_peers(send_turned)
    rot[mine, :] = turned[me]

    def z_rows(step):
        chunk = lax.rem(z + step + nz, nz) * 2 + core
        return wkv.at[pl.ds(pl.multiple_of(chunk * ck, ck), ck), :]

    def z_start():
        loads[2].wait()
        wait(wkv.at[pl.ds(0, ck), pl.ds(0, (N - 1) * KVB)], k_recv)
        part = z_rows(0)
        send(part, part, z_send, zr_recv.at[0], z_up)
        send(part, part, z_send, zl_recv.at[0], z_down)
        send(part, part, z_send, sib_recv, sibling)

    def z_step(s):
        part = z_rows(-s)
        wait(part, zr_recv.at[s - 1])
        if s < nz // 2:
            send(part, part, z_send, zr_recv.at[s], z_up)
        send(part, part, z_send, sib_recv, sibling)
        if s < nz // 2:
            part = z_rows(s)
            wait(part, zl_recv.at[s - 1])
            if s < nz // 2 - 1:
                send(part, part, z_send, zl_recv.at[s], z_down)
            send(part, part, z_send, sib_recv, sibling)

    z_todo = list(range(1, nz // 2 + 1))

    def z_next():
        if z_todo:
            z_step(z_todo.pop(0))

    def block(half, c, a):
        return (c, a) if half == 0 else (a, c)

    def row0(half, g):
        return g * GR + half * HR

    def matmul(dy, dx):
        w_loads[dy, dx].wait()
        pb[dy, dx] = jnp.dot(rot[...], w[dy, dx], preferred_element_type=F32).astype(BF16)

    def first_far(half, g, c):
        dy, dx = block(half, c, 2)
        r = row0(half, g)
        for way in range(2):
            send(
                pb.at[dy, dx, pl.ds(r + way * QR, QR), :], s1.at[half, g, c, way],
                p_send, s1_recv.at[half, g, c, way], along[half][way],
            )

    def first_near(half, g, c):
        r = row0(half, g)
        for way, a in enumerate((1, 3)):
            dy, dx = block(half, c, a)
            part = slice(r + way * QR, r + (way + 1) * QR)
            wait(s1.at[half, g, c, way], s1_recv.at[half, g, c, way])
            pb[dy, dx, part, :] = (
                pb[dy, dx, part, :].astype(F32) + s1[half, g, c, way].astype(F32)
            ).astype(BF16)
            send(
                pb.at[dy, dx, pl.ds(r, HR), :], f.at[half, g, c, way],
                p_send, f_recv.at[half, g, c, way], along[half][way],
            )

    def second(half, g, c):
        r = row0(half, g)
        dy, dx = block(half, c, 0)
        total = pb[dy, dx, r : r + HR, :].astype(F32)
        for way in range(2):
            wait(f.at[half, g, c, way], f_recv.at[half, g, c, way])
            total = total + f[half, g, c, way].astype(F32)
        if c == 0:
            own[half, g] = total
            return
        q[half, g, c - 1] = total.astype(BF16)
        if c == 2:
            for way in range(2):
                send(
                    q.at[half, g, 1, pl.ds(way * QR, QR), :], s1b.at[half, g, way],
                    q_send, s1b_recv.at[half, g, way], along[1 - half][way],
                )
            return
        way = 0 if c == 1 else 1
        part = slice(way * QR, (way + 1) * QR)
        wait(s1b.at[half, g, way], s1b_recv.at[half, g, way])
        q[half, g, c - 1, part, :] = (
            total[part, :] + s1b[half, g, way].astype(F32)
        ).astype(BF16)
        send(
            q.at[half, g, c - 1], fb.at[half, g, way],
            q_send, fb_recv.at[half, g, way], along[1 - half][way],
        )

    def residual_rows(g):
        out_scale = jnp.exp2(oe[...].astype(F32))
        gains = gn[...].astype(F32)
        squares = []
        for half in range(2):
            rows = slice(row0(half, g), row0(half, g) + HR)
            total = own[half, g]
            for way in range(2):
                wait(fb.at[half, g, way], fb_recv.at[half, g, way])
                total = total + fb[half, g, way].astype(F32)
            out = (res[rows, :].astype(F32) + total * out_scale).astype(BF16)
            ro[rows, :] = out
            hidden = out.astype(F32)
            xn[rows, :] = (hidden * gains).astype(BF16)
            squares.append(jnp.sum(hidden * hidden, axis=1, keepdims=True))
        column = jnp.concatenate(squares, axis=0)
        sqs[g] = jnp.transpose(jnp.broadcast_to(column, (GR, 128)))[:8, :]
        rows = pl.ds(g * GR, GR)
        pltpu.make_async_copy(ro.at[rows, :], resid_out.at[rows, :], out_sem.at[g]).start()

    def project(g):
        sqr[g, me] = sqs[g]

        def send_square(j):
            send(sqs.at[g], sqr.at[g, me], sq_send.at[g], sq_recv.at[g], {"tensor": j})

        to_peers(send_square)
        rows = slice(g * GR, (g + 1) * GR)
        for i in range(4):
            part = jnp.dot(
                xn[rows, :], wkv[:, i * 512 : (i + 1) * 512], preferred_element_type=F32
            ).astype(BF16)
            for k in range(4):
                kp[g, i * 4 + k] = part[:, k * KVB : (k + 1) * KVB]
        kr[g, me] = kp[g, me]

        def send_part(j):
            send(kp.at[g, j], kr.at[g, me], kv_send.at[g], kv_recv.at[g], {"tensor": j})

        to_peers(send_part)

    def finish(g):
        wait(sqr.at[g, pl.ds(0, N - 1)], sq_recv.at[g])
        total_sq = sqr[g, 0]
        for s in range(1, N):
            total_sq = total_sq + sqr[g, s]
        inv = lax.rsqrt(total_sq / D + 1e-05)
        scale = jnp.transpose(jnp.broadcast_to(inv[:1, :], (128, GR)))
        scale = scale * jnp.exp2(ke[...].astype(F32))
        wait(kr.at[g, pl.ds(0, N - 1)], kv_recv.at[g])
        total = kr[g, 0].astype(F32)
        for s in range(1, N):
            total = total + kr[g, s].astype(F32)
        ko[g * GR : (g + 1) * GR, :] = (total * scale).astype(BF16)
        rows = pl.ds(g * GR, GR)
        pltpu.make_async_copy(ko.at[rows, :], kv_out.at[rows, :], out_sem.at[GROUPS + g]).start()

    z_start()
    wait(rot.at[pl.ds(0, (N - 1) * 16), :], r_recv)

    matmul(2, 2)
    first_far(0, 0, 2)
    first_far(1, 0, 2)
    matmul(1, 2)
    first_far(0, 0, 1)
    matmul(2, 1)
    first_far(1, 0, 1)
    matmul(3, 2)
    first_far(0, 0, 3)
    matmul(2, 3)
    first_far(1, 0, 3)
    first_near(0, 0, 2)
    first_near(1, 0, 2)
    matmul(0, 2)
    first_far(0, 0, 0)
    matmul(2, 0)
    first_far(1, 0, 0)
    for dy, dx in ((1, 1), (1, 3), (3, 1), (3, 3)):
        matmul(dy, dx)
    z_next()
    for c in (1, 3):
        first_near(0, 0, c)
        first_near(1, 0, c)
    for dy, dx in ((0, 1), (0, 3), (1, 0), (3, 0)):
        matmul(dy, dx)
    first_near(0, 0, 0)
    first_near(1, 0, 0)
    matmul(0, 0)
    z_next()
    for c in CHUNKS:
        first_far(0, 1, c)
        first_far(1, 1, c)
    for i in range(3, 7):
        loads[i].wait()
    for c in CHUNKS:
        second(0, 0, c)
        second(1, 0, c)
        first_near(0, 1, c)
        first_near(1, 1, c)
        z_next()
    residual_rows(0)
    while z_todo:
        z_next()
    wait(wkv.at[pl.ds(0, BLK // 2), :], sib_recv)
    project(0)
    for c in CHUNKS:
        second(0, 1, c)
        second(1, 1, c)
    residual_rows(1)
    project(1)
    finish(0)
    finish(1)

    wait(att.at[pl.ds(0, N - 1)], a_send)
    wait(wkv.at[pl.ds(0, ck), pl.ds(0, (N - 1) * KVB)], k_send)
    wait(turned.at[pl.ds(0, N - 1)], r_send)
    wait(pb.at[pl.ds(0, 3)], p_send)
    wait(pb.at[0, pl.ds(0, 3)], q_send)
    wait(wkv.at[pl.ds(0, (nz - 1) * ck), :], z_send)
    wait(wkv.at[pl.ds(0, nz * ck), :], z_send)
    for g in range(GROUPS):
        wait(kp.at[g, pl.ds(0, N - 1)], kv_send.at[g])
        wait(sqr.at[g, pl.ds(0, N - 1)], sq_send.at[g])
        rows = pl.ds(g * GR, GR)
        pltpu.make_async_copy(ro.at[rows, :], resid_out.at[rows, :], out_sem.at[g]).wait()
        pltpu.make_async_copy(ko.at[rows, :], kv_out.at[rows, :], out_sem.at[GROUPS + g]).wait()


def body(n_dp, attn_out, head_signs, w_out, out_exp, residual, norm_gain, w_kv, kv_exp):
    vmem = pltpu.VMEM
    dma = pltpu.SemaphoreType.DMA
    half = BLK // n_dp
    nz = n_dp // 2
    scratch = [
        pltpu.SMEM((N * LH,), jnp.int32),
        vmem((N, 16, BLK), BF16),
        vmem((N, 16, BLK), F32),
        vmem((N, 16, BLK), BF16),
        vmem((TOK, BLK), BF16),
        vmem((4, 4, BLK, BLK), BF16),
        vmem((4, 4, TOK, BLK), BF16),
        vmem((2, GROUPS, 4, 2, QR, BLK), BF16),
        vmem((2, GROUPS, 4, 2, HR, BLK), BF16),
        vmem((2, GROUPS, 3, HR, BLK), BF16),
        vmem((2, GROUPS, HR, BLK), F32),
        vmem((2, GROUPS, 2, QR, BLK), BF16),
        vmem((2, GROUPS, 2, HR, BLK), BF16),
        vmem((BLK, N * KVB), BF16),
        vmem((TOK, BLK), BF16),
        vmem((GROUPS, N, GR, KVB), BF16),
        vmem((GROUPS, N, GR, KVB), BF16),
        vmem((GROUPS, 8, GR), F32),
        vmem((GROUPS, N, 8, GR), F32),
        vmem((TOK, BLK), BF16),
        vmem((TOK, BLK), BF16),
        vmem((1, BLK), BF16),
        vmem((1, BLK), jnp.int32),
        vmem((1, KVB), jnp.int32),
        vmem((TOK, KVB), BF16),
        dma((7,)),
        dma((16,)),
        dma((2 * GROUPS,)),
        dma, dma, dma, dma, dma, dma,
        dma,
        dma((2, GROUPS, 4, 2)),
        dma((2, GROUPS, 4, 2)),
        dma,
        dma((2, GROUPS, 2)),
        dma((2, GROUPS, 2)),
        dma,
        dma((nz // 2,)),
        dma((nz // 2,)),
        dma,
        dma((GROUPS,)), dma((GROUPS,)),
        dma((GROUPS,)), dma((GROUPS,)),
    ]
    anywhere = pl.BlockSpec(memory_space=pl.ANY)
    return pl.pallas_call(
        functools.partial(kernel, n_dp),
        out_shape=(
            jax.ShapeDtypeStruct((TOK, BLK), BF16),
            jax.ShapeDtypeStruct((TOK, KVB), BF16),
        ),
        in_specs=[anywhere] * 8,
        out_specs=(anywhere, anywhere),
        scratch_shapes=scratch,
        compiler_params=pltpu.CompilerParams(
            collective_id=0, has_side_effects=True, vmem_limit_bytes=48 * 1024 * 1024
        ),
    )(
        attn_out, head_signs, w_out, out_exp.reshape(1, BLK), residual,
        norm_gain.reshape(1, BLK), w_kv, kv_exp.reshape(1, KVB),
    )


def solution(mesh):
    placed = (
        P("dp", "tensor"),
        P(),
        P("tensor", None),
        P("tensor"),
        P("dp", "tensor"),
        P("tensor"),
        P(None, "tensor"),
        P("tensor"),
    )
    return jax.shard_map(
        functools.partial(body, mesh.shape["dp"]),
        mesh=mesh,
        in_specs=placed,
        out_specs=(P("dp", "tensor"), P("dp", "tensor")),
        check_vma=False,
    )
```

time: 279 us -> 92.6 us (0.33)
  waiting for transfers between devices: 194 us -> 0 us
  Pallas kernels: 0 us -> 82.7 us
  blocking collectives: 32.4 us -> 0 us
  starting transfers between devices: 16.9 us -> 0 us
  between operations: 14.2 us -> 0.64 us
  matrix products: 13.5 us -> 0 us
  local copies, waits for them, and re-layouts: 1.83 us -> 7.5 us
  other arithmetic: 5.46 us -> 0 us
    reduce_scatter x1 -> x0, waiting for transfers between devices: 96.5 us -> none  [body(): lax.psum_scatter(lax.dot_general(w_out, rotated, (((0,), (1,)), ((), ()))...]
    pallas_call x0 -> x1, Pallas kernels: none -> 82.7 us  [body(): pl.pallas_call(functools.partial(kernel, n_dp), out_shape=(jax.ShapeDtype...]
    all_gather x1 -> x0, waiting for transfers between devices: 75.3 us -> none  [body(): lax.all_gather(normed, 'tensor', axis=1, tiled=True)]
    psum x1 -> x0, blocking collectives: 32.4 us -> none  [body(): total_sq = lax.psum(partial_sq, 'tensor')]
    ppermute x4 -> x0, waiting for transfers between devices: 22.2 us -> none  [from_partner(): return lax.ppermute(block, axis, route)]
    ppermute x4 -> x0, starting transfers between devices: 16.8 us -> none  [from_partner(): return lax.ppermute(block, axis, route)]
    dot_general x3 -> x0, matrix products: 13.5 us -> none  [the longest x1 7.7 us: body(): lax.dot_general(w_out, rotated, (((0,), (1,)), ((), ())), preferred_eleme...]
    unnamed x12 -> x14, local copies, waits for them, and re-layouts: 0.63 us -> 6.81 us
  transfers between devices with their start and end apart: 6 -> 0, of which waited for: 6 -> 0; matrix products, arithmetic and copies ran while one was open for 0% -> 0% of each run, Pallas kernels for 0% -> 0%
where the time goes in v1:
time: 92.6 us; the launch traced here: 90.9 us
  Pallas kernels  82.7 us (89%)
  local copies, waits for them, and re-layouts  7.5 us (8%)
    pallas_call x1, Pallas kernels, body(): pl.pallas_call(functools.partial(kernel, n_dp), out_shape=(jax.ShapeDtype...  82.7 us
    unnamed x14, local copies, waits for them, and re-layouts  6.81 us

profile of v1, /device:TPU:6, one launch (start us, length us, event | category | flops | bytes accessed | tf_op | source)
XLA Modules:
  0.0 90.9 jit_solution(6372652561350701608)
XLA Ops:
  0.6 0.7 reshape.14.gain
  1.3 0.0 copy-start
  1.3 1.6 %copy-done = bf16[8192,128]{1,0:T(8,128)(2,1)S(1)} copy-done((bf16[8192,128]{1,0:T(8,128)(2,1)S(1)}, bf16[8192,128]{1,0:T(8,128)(2,1)}, u32[]{:S(2)}) %copy-start) | copy-done | bytes 2097176
  2.9 0.0 copy-start.1
  2.9 0.9 %copy-done.1 = bf16[256,512]{1,0:T(8,128)(2,1)S(1)} copy-done((bf16[256,512]{1,0:T(8,128)(2,1)S(1)}, bf16[256,512]{1,0:T(8,128)(2,1)}, u32[]{:S(2)}) %copy-start.1) | copy-done | bytes 262168
  3.9 0.0 copy-start.2
  3.9 0.9 %copy-done.2 = bf16[256,512]{1,0:T(8,128)(2,1)S(1)} copy-done((bf16[256,512]{1,0:T(8,128)(2,1)S(1)}, bf16[256,512]{1,0:T(8,128)(2,1)}, u32[]{:S(2)}) %copy-start.2) | copy-done | bytes 262168
  4.8 0.0 copy-start.3
  4.8 0.7 copy-done.3
  5.5 0.0 copy-start.4
  5.5 0.7 copy-done.4
  6.1 0.0 copy-start.5
  6.1 0.7 copy-done.5
  6.8 82.7 %shard_map.95 = (bf16[256,512]{1,0:T(8,128)(2,1)S(1)}, bf16[256,128]{1,0:T(8,128)(2,1)S(1)}) custom-call(bf16[256,512]{1,0:T(8,128)(2,1)S(1)} %copy-done.1, s32[64]{0:T(128)S(1)} %copy-done.4, bf16[512,8192]{1,0:T(8,128)(2,1)} %w_out.1, s32[1,512]{1,0:T(1,128)S(1)} %bitcast.2, bf16[256,512]{1,0:T(8,128)(2,1)S(1)} %copy-done.2, ...), custom_call_target="tpu_custom_call" | custom-call | tf_op jit(solution)/shard_map/pallas_call | solution.py:428
  89.6 0.7 copy.12
  90.3 0.6 copy.13
Async XLA Ops:
  1.3 1.6 %copy-start = (bf16[8192,128]{1,0:T(8,128)(2,1)S(1)}, bf16[8192,128]{1,0:T(8,128)(2,1)}, u32[]{:S(2)}) copy-start(bf16[8192,128]{1,0:T(8,128)(2,1)} %w_kv.1) | copy-start | bytes 6291460
  2.9 0.9 %copy-start.1 = (bf16[256,512]{1,0:T(8,128)(2,1)S(1)}, bf16[256,512]{1,0:T(8,128)(2,1)}, u32[]{:S(2)}) copy-start(bf16[256,512]{1,0:T(8,128)(2,1)} %attn.1) | copy-start | bytes 786436
  3.9 0.9 %copy-start.2 = (bf16[256,512]{1,0:T(8,128)(2,1)S(1)}, bf16[256,512]{1,0:T(8,128)(2,1)}, u32[]{:S(2)}) copy-start(bf16[256,512]{1,0:T(8,128)(2,1)} %residual.1) | copy-start | bytes 786436
  4.8 0.7 copy-start.3
  5.5 0.7 copy-start.4
  6.1 0.7 copy-start.5

commit v2 on v1

v2 whole, which is shorter than its diff:
```python
import jax
import jax.numpy as jnp
from jax import lax
from jax.experimental import pallas as pl
from jax.experimental.pallas import tpu as pltpu
from jax.sharding import PartitionSpec as P

MESH = pl.DeviceIdType.MESH
BF16 = jnp.bfloat16
F32 = jnp.float32
HD = 128
LH = 4
N = 16
TOK = 256
BLK = 512
D = N * BLK
KVB = 128
GROUPS = ((0, 128), (128, 64), (192, 64))
SQW = 128
PLANES = 4
SHARES = 2 * PLANES
CK = BLK // SHARES
CHUNKS = (2, 1, 3, 0)
ORDER = (
    (2, 2), (1, 2), (2, 1), (3, 2), (2, 3), (0, 2), (2, 0), (1, 1),
    (1, 3), (3, 1), (3, 3), (0, 1), (0, 3), (1, 0), (3, 0), (0, 0),
)


def hadamard(vals):
    step = 1
    while step < len(vals):
        out = list(vals)
        for i in range(len(vals)):
            if not i & step:
                out[i] = vals[i] + vals[i | step]
                out[i | step] = vals[i] - vals[i | step]
        vals = out
        step *= 2
    return vals


def kernel(
    attn, signs, w_out, out_exp, residual, gain, w_kv, kv_exp,
    resid_out, kv_out,
    sgn, att, mixed, turned, rot, w, pb, s1, f, q, own, s1b, fb,
    wkv, xn, kp, kr, sqs, sqr, res, ro, gn, oe, ke, ko,
    in_sem, w_sem, out_sem,
    a_send, a_recv, k_send, k_recv, r_send, r_recv,
    p_send, s1_recv, f_recv, q_send, s1b_recv, fb_recv,
    z_send, z_recv, sib_send, sib_recv,
    kv_send, kv_recv, sq_send, sq_recv,
):
    me = lax.axis_index("tensor")
    dp = lax.axis_index("dp")
    y, x = me // 4, lax.rem(me, 4)
    z, core = dp // 2, lax.rem(dp, 2)
    plane = lax.rem(z, PLANES)
    share = core * PLANES + plane

    def at_yx(dy, dx):
        return lax.rem(y + dy, 4) * 4 + lax.rem(x + dx, 4)

    along = (
        ({"tensor": at_yx(0, 1)}, {"tensor": at_yx(0, 3)}),
        ({"tensor": at_yx(1, 0)}, {"tensor": at_yx(3, 0)}),
    )
    z_peers = [
        {"dp": (z - plane + lax.rem(plane + k, PLANES)) * 2 + core} for k in range(1, PLANES)
    ]
    sibling = {"dp": z * 2 + 1 - core}

    def send(src, dst, send_sem, recv_sem, to):
        pltpu.make_async_remote_copy(
            src_ref=src, dst_ref=dst, send_sem=send_sem, recv_sem=recv_sem,
            device_id=to, device_id_type=MESH,
        ).start()

    def wait(ref, sem):
        pltpu.make_async_copy(ref, ref, sem).wait()

    def to_peers(fn):
        def one(k, carry):
            fn(lax.rem(me + k, N))
            return carry

        lax.fori_loop(1, N, one, 0)

    mine = pl.ds(pl.multiple_of(me * 16, 16), 16)
    my_rows = pl.ds(pl.multiple_of(share * CK, CK), CK)
    my_cols = pl.ds(pl.multiple_of(me * KVB, KVB), KVB)
    loads = [
        pltpu.make_async_copy(attn.at[mine, :], att.at[me], in_sem.at[0]),
        pltpu.make_async_copy(signs, sgn, in_sem.at[1]),
        pltpu.make_async_copy(
            w_kv.at[pl.ds(pl.multiple_of(me * BLK + share * CK, CK), CK), :],
            wkv.at[my_rows, my_cols], in_sem.at[2],
        ),
        pltpu.make_async_copy(out_exp, oe, in_sem.at[3]),
        pltpu.make_async_copy(residual, res, in_sem.at[4]),
        pltpu.make_async_copy(gain, gn, in_sem.at[5]),
        pltpu.make_async_copy(kv_exp, ke, in_sem.at[6]),
    ]
    for copy in loads:
        copy.start()

    w_loads = {}
    for i, (dy, dx) in enumerate(ORDER):
        columns = pl.ds(pl.multiple_of(at_yx(dy, dx) * BLK, BLK), BLK)
        w_loads[dy, dx] = pltpu.make_async_copy(w_out.at[:, columns], w.at[dy, dx], w_sem.at[i])

    barrier = pltpu.get_barrier_semaphore()

    def greet(j):
        pl.semaphore_signal(barrier, inc=1, device_id={"tensor": j}, device_id_type=MESH)

    to_peers(greet)
    for to in (*z_peers, sibling):
        pl.semaphore_signal(barrier, inc=1, device_id=to, device_id_type=MESH)
    pl.semaphore_wait(barrier, N - 1 + PLANES)

    def send_tokens(j):
        rows = pl.ds(pl.multiple_of(j * 16, 16), 16)
        send(attn.at[rows, :], att.at[me], a_send, a_recv, {"tensor": j})

    to_peers(send_tokens)

    def send_kv_rows(j):
        rows = pl.ds(pl.multiple_of(j * BLK + share * CK, CK), CK)
        send(w_kv.at[rows, :], wkv.at[my_rows, my_cols], k_send, k_recv, {"tensor": j})

    to_peers(send_kv_rows)
    for dy, dx in ORDER:
        w_loads[dy, dx].start()

    loads[0].wait()
    loads[1].wait()
    wait(att.at[pl.ds(0, N - 1)], a_recv)
    for s in range(N):
        heads = []
        for h in range(LH):
            sign = (2 * sgn[s * LH + h] - 1).astype(F32)
            heads.append(att[s, :, h * HD : (h + 1) * HD].astype(F32) * sign)
        for h, val in enumerate(hadamard(heads)):
            mixed[s, :, h * HD : (h + 1) * HD] = val
    for h in range(LH):
        at = slice(h * HD, (h + 1) * HD)
        for g, val in enumerate(hadamard([mixed[s, :, at] for s in range(N)])):
            turned[g, :, at] = (val * 0.125).astype(BF16)

    def send_turned(j):
        send(turned.at[j], rot.at[mine, :], r_send, r_recv, {"tensor": j})

    to_peers(send_turned)
    rot[mine, :] = turned[me]

    def z_start():
        loads[2].wait()
        wait(wkv.at[pl.ds(0, CK), pl.ds(0, (N - 1) * KVB)], k_recv)
        part = wkv.at[my_rows, :]
        for to in z_peers:
            send(part, part, z_send, z_recv, to)

    def z_finish():
        wait(wkv.at[pl.ds(0, (PLANES - 1) * CK), :], z_recv)
        rows = pl.ds(pl.multiple_of(core * (BLK // 2), BLK // 2), BLK // 2)
        send(wkv.at[rows, :], wkv.at[rows, :], sib_send, sib_recv, sibling)

    def block(half, c, a):
        return (c, a) if half == 0 else (a, c)

    def half_rows(half, g):
        start, size = GROUPS[g]
        return start + half * (size // 2), size // 2

    def matmul(dy, dx):
        w_loads[dy, dx].wait()
        pb[dy, dx] = jnp.dot(rot[...], w[dy, dx], preferred_element_type=F32).astype(BF16)

    def first_far(half, g, c):
        dy, dx = block(half, c, 2)
        r, size = half_rows(half, g)
        qr, slot = size // 2, pl.ds(GROUPS[g][0] // 4, size // 2)
        for way in range(2):
            send(
                pb.at[dy, dx, pl.ds(r + way * qr, qr), :], s1.at[half, c, way, slot, :],
                p_send, s1_recv.at[half, g, c, way], along[half][way],
            )

    def first_near(half, g, c):
        r, size = half_rows(half, g)
        qr, at = size // 2, GROUPS[g][0] // 4
        slot = pl.ds(GROUPS[g][0] // 2, size)
        for way, a in enumerate((1, 3)):
            dy, dx = block(half, c, a)
            part = slice(r + way * qr, r + (way + 1) * qr)
            wait(s1.at[half, c, way, pl.ds(at, qr), :], s1_recv.at[half, g, c, way])
            pb[dy, dx, part, :] = (
                pb[dy, dx, part, :].astype(F32) + s1[half, c, way, at : at + qr, :].astype(F32)
            ).astype(BF16)
            send(
                pb.at[dy, dx, pl.ds(r, size), :], f.at[half, c, way, slot, :],
                p_send, f_recv.at[half, g, c, way], along[half][way],
            )

    def second(half, g, c):
        r, size = half_rows(half, g)
        qr, at, far = size // 2, GROUPS[g][0] // 2, GROUPS[g][0] // 4
        slot = pl.ds(at, size)
        dy, dx = block(half, c, 0)
        total = pb[dy, dx, r : r + size, :].astype(F32)
        for way in range(2):
            wait(f.at[half, c, way, slot, :], f_recv.at[half, g, c, way])
            total = total + f[half, c, way, at : at + size, :].astype(F32)
        if c == 0:
            own[half, at : at + size, :] = total
            return
        if c == 2:
            q[half, 1, at : at + size, :] = total.astype(BF16)
            for way in range(2):
                send(
                    q.at[half, 1, pl.ds(at + way * qr, qr), :], s1b.at[half, way, pl.ds(far, qr), :],
                    q_send, s1b_recv.at[half, g, way], along[1 - half][way],
                )
            return
        way = 0 if c == 1 else 1
        part = slice(way * qr, (way + 1) * qr)
        rest = slice((1 - way) * qr, (2 - way) * qr)
        q[half, c - 1, at + rest.start : at + rest.stop, :] = total[rest, :].astype(BF16)
        wait(s1b.at[half, way, pl.ds(far, qr), :], s1b_recv.at[half, g, way])
        q[half, c - 1, at + part.start : at + part.stop, :] = (
            total[part, :] + s1b[half, way, far : far + qr, :].astype(F32)
        ).astype(BF16)
        send(
            q.at[half, c - 1, slot, :], fb.at[half, way, slot, :],
            q_send, fb_recv.at[half, g, way], along[1 - half][way],
        )

    def residual_rows(g):
        start, group = GROUPS[g]
        at = start // 2
        out_scale = jnp.exp2(oe[...].astype(F32))
        gains = gn[...].astype(F32).reshape(1, BLK)
        squares = []
        for half in range(2):
            r, size = half_rows(half, g)
            rows = slice(r, r + size)
            total = own[half, at : at + size, :]
            for way in range(2):
                wait(fb.at[half, way, pl.ds(at, size), :], fb_recv.at[half, g, way])
                total = total + fb[half, way, at : at + size, :].astype(F32)
            out = (res[rows, :].astype(F32) + total * out_scale).astype(BF16)
            ro[rows, :] = out
            hidden = out.astype(F32)
            xn[rows, :] = (hidden * gains).astype(BF16)
            squares.append(jnp.sum(hidden * hidden, axis=1, keepdims=True))
        if group < SQW:
            squares.append(jnp.zeros((SQW - group, 1), F32))
        column = jnp.concatenate(squares, axis=0)
        sqs[g] = jnp.transpose(jnp.broadcast_to(column, (SQW, 128)))[:8, :]
        rows = pl.ds(start, group)
        pltpu.make_async_copy(ro.at[rows, :], resid_out.at[rows, :], out_sem.at[g]).start()

    def project(g):
        start, group = GROUPS[g]
        rows = slice(start, start + group)
        sqr[g, me] = sqs[g]

        def send_square(j):
            send(sqs.at[g], sqr.at[g, me], sq_send.at[g], sq_recv.at[g], {"tensor": j})

        to_peers(send_square)
        for i in range(4):
            part = jnp.dot(
                xn[rows, :], wkv[:, i * 512 : (i + 1) * 512], preferred_element_type=F32
            ).astype(BF16)
            for k in range(4):
                kp[i * 4 + k, rows, :] = part[:, k * KVB : (k + 1) * KVB]
        kr[me, rows, :] = kp[me, rows, :]
        slot = pl.ds(start, group)

        def send_part(j):
            send(
                kp.at[j, slot, :], kr.at[me, slot, :],
                kv_send.at[g], kv_recv.at[g], {"tensor": j},
            )

        to_peers(send_part)

    def finish(g):
        start, group = GROUPS[g]
        rows = slice(start, start + group)
        wait(sqr.at[g, pl.ds(0, N - 1)], sq_recv.at[g])
        total_sq = sqr[g, 0]
        for s in range(1, N):
            total_sq = total_sq + sqr[g, s]
        inv = lax.rsqrt(total_sq / D + 1e-05)
        scale = jnp.transpose(jnp.broadcast_to(inv[:1, :], (128, SQW)))[:group, :]
        scale = scale * jnp.exp2(ke[...].astype(F32))
        wait(kr.at[pl.ds(0, N - 1), pl.ds(start, group), :], kv_recv.at[g])
        total = kr[0, rows, :].astype(F32)
        for s in range(1, N):
            total = total + kr[s, rows, :].astype(F32)
        ko[rows, :] = (total * scale).astype(BF16)
        out = pl.ds(start, group)
        pltpu.make_async_copy(ko.at[out, :], kv_out.at[out, :], out_sem.at[len(GROUPS) + g]).start()

    z_start()
    wait(rot.at[pl.ds(0, (N - 1) * 16), :], r_recv)

    matmul(2, 2)
    first_far(0, 0, 2)
    first_far(1, 0, 2)
    matmul(1, 2)
    first_far(0, 0, 1)
    matmul(2, 1)
    first_far(1, 0, 1)
    matmul(3, 2)
    first_far(0, 0, 3)
    matmul(2, 3)
    first_far(1, 0, 3)
    first_near(0, 0, 2)
    first_near(1, 0, 2)
    matmul(0, 2)
    first_far(0, 0, 0)
    matmul(2, 0)
    first_far(1, 0, 0)
    for dy, dx in ((1, 1), (1, 3), (3, 1), (3, 3)):
        matmul(dy, dx)
    for c in (1, 3):
        first_near(0, 0, c)
        first_near(1, 0, c)
    for dy, dx in ((0, 1), (0, 3), (1, 0), (3, 0)):
        matmul(dy, dx)
    first_near(0, 0, 0)
    first_near(1, 0, 0)
    matmul(0, 0)
    for i in range(3, 7):
        loads[i].wait()
    last = len(GROUPS) - 1
    for g in range(last + 1):
        if g < last:
            for c in CHUNKS:
                first_far(0, g + 1, c)
                first_far(1, g + 1, c)
        for c in CHUNKS:
            second(0, g, c)
            second(1, g, c)
            if g < last:
                first_near(0, g + 1, c)
                first_near(1, g + 1, c)
            if g == 1 and c == 2:
                z_finish()
            if g > 0 and c == 3:
                if g == 1:
                    wait(wkv.at[pl.ds(0, BLK // 2), :], sib_recv)
                project(g - 1)
        residual_rows(g)
    project(last)
    for g in range(last + 1):
        finish(g)

    wait(att.at[pl.ds(0, N - 1)], a_send)
    wait(wkv.at[pl.ds(0, CK), pl.ds(0, (N - 1) * KVB)], k_send)
    wait(turned.at[pl.ds(0, N - 1)], r_send)
    wait(pb.at[pl.ds(0, 3)], p_send)
    wait(pb.at[0, pl.ds(0, 3)], q_send)
    wait(wkv.at[pl.ds(0, (PLANES - 1) * CK), :], z_send)
    wait(wkv.at[pl.ds(0, BLK // 2), :], sib_send)
    for g, (start, group) in enumerate(GROUPS):
        rows = pl.ds(start, group)
        wait(kp.at[pl.ds(0, N - 1), rows, :], kv_send.at[g])
        wait(sqr.at[g, pl.ds(0, N - 1)], sq_send.at[g])
        pltpu.make_async_copy(ro.at[rows, :], resid_out.at[rows, :], out_sem.at[g]).wait()
        pltpu.make_async_copy(
            ko.at[rows, :], kv_out.at[rows, :], out_sem.at[len(GROUPS) + g]
        ).wait()


def body(attn_out, head_signs, w_out, out_exp, residual, norm_gain, w_kv, kv_exp):
    vmem = pltpu.VMEM
    dma = pltpu.SemaphoreType.DMA
    groups = len(GROUPS)
    scratch = [
        pltpu.SMEM((N * LH,), jnp.int32),
        vmem((N, 16, BLK), BF16),
        vmem((N, 16, BLK), F32),
        vmem((N, 16, BLK), BF16),
        vmem((TOK, BLK), BF16),
        vmem((4, 4, BLK, BLK), BF16),
        vmem((4, 4, TOK, BLK), BF16),
        vmem((2, 4, 2, TOK // 4, BLK), BF16),
        vmem((2, 4, 2, TOK // 2, BLK), BF16),
        vmem((2, 3, TOK // 2, BLK), BF16),
        vmem((2, TOK // 2, BLK), F32),
        vmem((2, 2, TOK // 4, BLK), BF16),
        vmem((2, 2, TOK // 2, BLK), BF16),
        vmem((BLK, N * KVB), BF16),
        vmem((TOK, BLK), BF16),
        vmem((N, TOK, KVB), BF16),
        vmem((N, TOK, KVB), BF16),
        vmem((groups, 8, SQW), F32),
        vmem((groups, N, 8, SQW), F32),
        vmem((TOK, BLK), BF16),
        vmem((TOK, BLK), BF16),
        vmem((BLK,), BF16),
        vmem((1, BLK), jnp.int32),
        vmem((1, KVB), jnp.int32),
        vmem((TOK, KVB), BF16),
        dma((7,)),
        dma((16,)),
        dma((2 * groups,)),
        dma, dma, dma, dma, dma, dma,
        dma,
        dma((2, groups, 4, 2)),
        dma((2, groups, 4, 2)),
        dma,
        dma((2, groups, 2)),
        dma((2, groups, 2)),
        dma, dma, dma, dma,
        dma((groups,)), dma((groups,)),
        dma((groups,)), dma((groups,)),
    ]
    anywhere = pl.BlockSpec(memory_space=pl.ANY)
    return pl.pallas_call(
        kernel,
        out_shape=(
            jax.ShapeDtypeStruct((TOK, BLK), BF16),
            jax.ShapeDtypeStruct((TOK, KVB), BF16),
        ),
        in_specs=[anywhere] * 8,
        out_specs=(anywhere, anywhere),
        scratch_shapes=scratch,
        compiler_params=pltpu.CompilerParams(
            collective_id=0, has_side_effects=True, vmem_limit_bytes=62 * 1024 * 1024
        ),
    )(
        attn_out, head_signs, w_out, out_exp.reshape(1, BLK), residual,
        norm_gain, w_kv, kv_exp.reshape(1, KVB),
    )


def solution(mesh):
    placed = (
        P("dp", "tensor"),
        P(),
        P("tensor", None),
        P("tensor"),
        P("dp", "tensor"),
        P("tensor"),
        P(None, "tensor"),
        P("tensor"),
    )
    return jax.shard_map(
        body,
        mesh=mesh,
        in_specs=placed,
        out_specs=(P("dp", "tensor"), P("dp", "tensor")),
        check_vma=False,
    )
```

time: 92.6 us -> 72.9 us (0.79); the launches traced: 90.9 us -> 72.3 us
  Pallas kernels: 82.7 us -> 68.5 us
  local copies, waits for them, and re-layouts: 7.5 us -> 3.14 us
    pallas_call x1, Pallas kernels: 82.7 us -> 68.5 us  [body(): pl.pallas_call(kernel, out_shape=(jax.ShapeDtypeStruct((TOK, BLK), BF16),...]
    unnamed x14 -> x2, local copies, waits for them, and re-layouts: 6.81 us -> 3.14 us
where the time goes in v2:
time: 72.9 us; the launch traced here: 72.3 us
  Pallas kernels  68.5 us (94%)
  local copies, waits for them, and re-layouts  3.14 us (4%)
    pallas_call x1, Pallas kernels, body(): pl.pallas_call(kernel, out_shape=(jax.ShapeDtypeStruct((TOK, BLK), BF16),...  68.5 us
    unnamed x2, local copies, waits for them, and re-layouts  3.14 us

profile of v2, /device:TPU:6, one launch (start us, length us, event | category | flops | bytes accessed | tf_op | source)
XLA Modules:
  0.0 72.3 jit_solution(6687641110709426785)
XLA Ops:
  0.6 68.5 %shard_map.95 = (bf16[256,512]{1,0:T(8,128)(2,1)}, bf16[256,128]{1,0:T(8,128)(2,1)}) custom-call(bf16[256,512]{1,0:T(8,128)(2,1)} %attn.1, s32[64]{0:T(128)} %signs.1, bf16[512,8192]{1,0:T(8,128)(2,1)} %w_out.1, s32[1,512]{1,0:T(1,128)} %bitcast.2, bf16[256,512]{1,0:T(8,128)(2,1)} %residual.1, bf16[512]{0:T(512)(128)(2,1)} %gain.1, bf16[8192,128]{1,0:T(8,128)(2,1)} %w_kv.1, ...), custom_call_target="tpu_custom_call" | custom-call | tf_op jit(solution)/shard_map/pallas_call | solution.py:425
  69.2 1.7 %copy.12 = bf16[256,512]{1,0:T(8,128)(2,1)} copy(bf16[256,512]{1,0:T(8,128)(2,1)} %get-tuple-element.4) | data formatting | bytes 524288
  70.8 1.5 %copy.13 = bf16[256,128]{1,0:T(8,128)(2,1)} copy(bf16[256,128]{1,0:T(8,128)(2,1)} %get-tuple-element.5) | data formatting | bytes 131072

commit v3 on v2

v3 whole, which is shorter than its diff:
```python
import jax
import jax.numpy as jnp
from jax import lax
from jax.experimental import pallas as pl
from jax.experimental.pallas import tpu as pltpu
from jax.sharding import PartitionSpec as P

MESH = pl.DeviceIdType.MESH
BF16 = jnp.bfloat16
F32 = jnp.float32
HD = 128
LH = 4
N = 16
TOK = 256
BLK = 512
D = N * BLK
KVB = 128
HALF = TOK // 2
HCOL = BLK // 2
GROUPS = ((0, 64), (64, 32), (96, 32))
LANES = 128
PLANES = 4
SHARES = 2 * PLANES
CK = BLK // SHARES
PEERS = (
    (2, 2), (2, 1), (1, 2), (2, 3), (3, 2), (2, 0), (0, 2), (1, 1),
    (3, 3), (1, 3), (3, 1), (0, 1), (1, 0), (0, 3), (3, 0),
)
CHUNKS = (2, 1, 3, 0)
ORDER = (
    (2, 2), (1, 2), (2, 1), (3, 2), (2, 3), (0, 2), (2, 0), (1, 1),
    (1, 3), (3, 1), (3, 3), (0, 1), (0, 3), (1, 0), (3, 0), (0, 0),
)


def hadamard(vals):
    step = 1
    while step < len(vals):
        out = list(vals)
        for i in range(len(vals)):
            if not i & step:
                out[i] = vals[i] + vals[i | step]
                out[i | step] = vals[i] - vals[i | step]
        vals = out
        step *= 2
    return vals


def kernel(
    attn, signs, w_out, out_exp, residual, gain, w_kv, kv_exp,
    resid_out, kv_out,
    sgn, att, mixed, turned, rot, w, pb, s1, f, q, own, s1b, fb,
    wkv, xn, res, ro, gn, oe, ke, ko, kp, kr,
    in_sem, w_sem, out_sem,
    a_send, a_recv, k_send, k_recv, r_send, r_recv,
    p_send, s1_recv, f_recv, q_send, s1b_recv, fb_recv,
    z_send, z_recv, sib_send, sib_recv,
    kv_send, kv_recv,
):
    me = lax.axis_index("tensor")
    dp = lax.axis_index("dp")
    y, x = me // 4, lax.rem(me, 4)
    z, core = dp // 2, lax.rem(dp, 2)
    plane = lax.rem(z, PLANES)
    share = core * PLANES + plane

    def at_yx(dy, dx):
        return lax.rem(y + dy, 4) * 4 + lax.rem(x + dx, 4)

    along = (
        ({"tensor": at_yx(0, 1)}, {"tensor": at_yx(0, 3)}),
        ({"tensor": at_yx(1, 0)}, {"tensor": at_yx(3, 0)}),
    )
    z_peers = [
        {"dp": (z - plane + lax.rem(plane + k, PLANES)) * 2 + core} for k in range(1, PLANES)
    ]
    sibling = {"dp": z * 2 + 1 - core}

    def send(src, dst, send_sem, recv_sem, to):
        pltpu.make_async_remote_copy(
            src_ref=src, dst_ref=dst, send_sem=send_sem, recv_sem=recv_sem,
            device_id=to, device_id_type=MESH,
        ).start()

    def wait(ref, sem):
        pltpu.make_async_copy(ref, ref, sem).wait()

    def to_peers(fn):
        for dy, dx in PEERS:
            fn(at_yx(dy, dx))

    barrier = pltpu.get_barrier_semaphore()

    def greet(j):
        pl.semaphore_signal(barrier, inc=1, device_id={"tensor": j}, device_id_type=MESH)

    to_peers(greet)
    for to in (*z_peers, sibling):
        pl.semaphore_signal(barrier, inc=1, device_id=to, device_id_type=MESH)

    mine = pl.ds(pl.multiple_of(me * 16, 16), 16)
    my_rows = pl.ds(pl.multiple_of(share * CK, CK), CK)
    my_cols = pl.ds(pl.multiple_of(me * KVB, KVB), KVB)
    loads = [
        pltpu.make_async_copy(attn.at[mine, :], att.at[me], in_sem.at[0]),
        pltpu.make_async_copy(signs, sgn, in_sem.at[1]),
        pltpu.make_async_copy(
            w_kv.at[pl.ds(pl.multiple_of(me * BLK + share * CK, CK), CK), :],
            wkv.at[my_rows, my_cols], in_sem.at[2],
        ),
        pltpu.make_async_copy(out_exp, oe, in_sem.at[3]),
        pltpu.make_async_copy(residual, res, in_sem.at[4]),
        pltpu.make_async_copy(gain, gn, in_sem.at[5]),
        pltpu.make_async_copy(kv_exp, ke, in_sem.at[6]),
    ]
    for copy in loads:
        copy.start()

    w_loads = {}
    for i, (dy, dx) in enumerate(ORDER):
        columns = pl.ds(pl.multiple_of(at_yx(dy, dx) * BLK, BLK), BLK)
        w_loads[dy, dx] = pltpu.make_async_copy(w_out.at[:, columns], w.at[dy, dx], w_sem.at[i])

    pl.semaphore_wait(barrier, N - 1 + PLANES)

    def send_tokens(j):
        rows = pl.ds(pl.multiple_of(j * 16, 16), 16)
        send(attn.at[rows, :], att.at[me], a_send, a_recv, {"tensor": j})

    to_peers(send_tokens)

    def send_kv_rows(j):
        rows = pl.ds(pl.multiple_of(j * BLK + share * CK, CK), CK)
        send(w_kv.at[rows, :], wkv.at[my_rows, my_cols], k_send, k_recv, {"tensor": j})

    to_peers(send_kv_rows)
    for dy, dx in ORDER:
        w_loads[dy, dx].start()

    loads[0].wait()
    loads[1].wait()
    wait(att.at[pl.ds(0, N - 1)], a_recv)
    for s in range(N):
        heads = []
        for h in range(LH):
            sign = (2 * sgn[s * LH + h] - 1).astype(F32)
            heads.append(att[s, :, h * HD : (h + 1) * HD].astype(F32) * sign)
        for h, val in enumerate(hadamard(heads)):
            mixed[s, :, h * HD : (h + 1) * HD] = val
    for h in range(LH):
        at = slice(h * HD, (h + 1) * HD)
        for g, val in enumerate(hadamard([mixed[s, :, at] for s in range(N)])):
            turned[g, :, at] = (val * 0.125).astype(BF16)

    def send_turned(j):
        send(turned.at[j], rot.at[mine, :], r_send, r_recv, {"tensor": j})

    to_peers(send_turned)
    rot[mine, :] = turned[me]

    def z_start():
        loads[2].wait()
        wait(wkv.at[pl.ds(0, CK), pl.ds(0, (N - 1) * KVB)], k_recv)
        part = wkv.at[my_rows, :]
        for to in z_peers:
            send(part, part, z_send, z_recv, to)

    def z_finish():
        wait(wkv.at[pl.ds(0, (PLANES - 1) * CK), :], z_recv)
        rows = pl.ds(pl.multiple_of(core * (BLK // 2), BLK // 2), BLK // 2)
        send(wkv.at[rows, :], wkv.at[rows, :], sib_send, sib_recv, sibling)

    def block(half, c, a):
        return (c, a) if half == 0 else (a, c)

    def rows_of(half, g):
        start, size = GROUPS[g]
        return pl.ds(half * HALF + start, size)

    def matmul(dy, dx):
        w_loads[dy, dx].wait()
        pb[dy, dx] = jnp.dot(rot[...], w[dy, dx], preferred_element_type=F32).astype(BF16)

    def first_far(half, c):
        dy, dx = block(half, c, 2)
        for way in range(2):
            send(
                pb.at[dy, dx, pl.ds(half * HALF, HALF), pl.ds(way * HCOL, HCOL)],
                s1.at[half, c, way], p_send, s1_recv.at[half, c, way], along[half][way],
            )

    def first_near(half, g, c):
        start, size = GROUPS[g]
        slot, rows = pl.ds(start, size), rows_of(half, g)
        for way, a in enumerate((1, 3)):
            dy, dx = block(half, c, a)
            part = pl.ds(way * HCOL, HCOL)
            if g == 0:
                wait(s1.at[half, c, way], s1_recv.at[half, c, way])
            pb[dy, dx, rows, part] = (
                pb[dy, dx, rows, part].astype(F32) + s1[half, c, way, slot, :].astype(F32)
            ).astype(BF16)
            send(
                pb.at[dy, dx, rows, :], f.at[half, c, way, slot, :],
                p_send, f_recv.at[half, g, c, way], along[half][way],
            )

    def second(half, g, c):
        start, size = GROUPS[g]
        slot, rows = pl.ds(start, size), rows_of(half, g)
        dy, dx = block(half, c, 0)
        total = pb[dy, dx, rows, :].astype(F32)
        for way in range(2):
            wait(f.at[half, c, way, slot, :], f_recv.at[half, g, c, way])
            total = total + f[half, c, way, slot, :].astype(F32)
        if c == 0:
            own[half, slot, :] = total
            return
        if c == 2:
            q[half, 1, slot, :] = total.astype(BF16)
            for way in range(2):
                send(
                    q.at[half, 1, slot, pl.ds(way * HCOL, HCOL)], s1b.at[half, way, slot, :],
                    q_send, s1b_recv.at[half, g, way], along[1 - half][way],
                )
            return
        way = 0 if c == 1 else 1
        part = slice(way * HCOL, (way + 1) * HCOL)
        rest = slice((1 - way) * HCOL, (2 - way) * HCOL)
        q[half, c - 1, slot, rest] = total[:, rest].astype(BF16)
        wait(s1b.at[half, way, slot, :], s1b_recv.at[half, g, way])
        q[half, c - 1, slot, part] = (
            total[:, part] + s1b[half, way, slot, :].astype(F32)
        ).astype(BF16)
        send(
            q.at[half, c - 1, slot, :], fb.at[half, way, slot, :],
            q_send, fb_recv.at[half, g, way], along[1 - half][way],
        )

    def residual_rows(g):
        start, size = GROUPS[g]
        slot = pl.ds(start, size)
        out_scale = jnp.exp2(oe[...].astype(F32))
        gains = gn[...].astype(F32).reshape(1, BLK)
        squares = []
        for half in range(2):
            rows = rows_of(half, g)
            total = own[half, slot, :]
            for way in range(2):
                wait(fb.at[half, way, slot, :], fb_recv.at[half, g, way])
                total = total + fb[half, way, slot, :].astype(F32)
            out = (res[rows, :].astype(F32) + total * out_scale).astype(BF16)
            ro[rows, :] = out
            hidden = out.astype(F32)
            xn[pl.ds(2 * start + half * size, size), :] = (hidden * gains).astype(BF16)
            squares.append(jnp.sum(hidden * hidden, axis=1, keepdims=True))
            pltpu.make_async_copy(ro.at[rows, :], resid_out.at[rows, :], out_sem.at[2 * g + half]).start()
        if 2 * size < LANES:
            squares.append(jnp.zeros((LANES - 2 * size, 1), F32))
        column = jnp.concatenate(squares, axis=0)
        row = jnp.transpose(jnp.broadcast_to(column, (LANES, LANES)))[:16, :]
        high = row.astype(BF16).astype(F32)
        mid = (row - high).astype(BF16).astype(F32)
        low = row - high - mid
        index = lax.broadcasted_iota(jnp.int32, (16, LANES), 0)
        return jnp.where(index == 0, high, jnp.where(index == 1, mid, jnp.where(index == 2, low, 0.0)))

    def project(g, squares):
        start, size = GROUPS[g]
        squares = squares.astype(BF16)
        hidden = xn[pl.ds(2 * start, 2 * size), :]
        for i in CHUNKS:
            yy = lax.rem(y + i, 4)
            columns = pl.ds(pl.multiple_of(yy * 4 * KVB, 4 * KVB), 4 * KVB)
            part = jnp.dot(hidden, wkv[:, columns], preferred_element_type=F32).astype(BF16)
            for k in range(4):
                kp[g][yy * 4 + k, : 2 * size, :] = part[:, k * KVB : (k + 1) * KVB]
                kp[g][yy * 4 + k, 2 * size :, :] = squares
            for k in CHUNKS:
                if i or k:
                    j = at_yx(i, k)
                    send(kp[g].at[j], kr[g].at[me], kv_send.at[g], kv_recv.at[g], {"tensor": j})
        kr[g][me] = kp[g][me]

    def finish(g):
        start, size = GROUPS[g]
        wait(kr[g].at[pl.ds(0, N - 1)], kv_recv.at[g])
        total = kr[g][0].astype(F32)
        for s in range(1, N):
            total = total + kr[g][s].astype(F32)
        at = 2 * size
        total_sq = total[at : at + 1, :] + total[at + 1 : at + 2, :] + total[at + 2 : at + 3, :]
        inv = lax.rsqrt(total_sq / D + 1e-05)
        scale = jnp.transpose(jnp.broadcast_to(inv, (LANES, LANES)))[:at, :]
        out = (total[:at, :] * scale * jnp.exp2(ke[...].astype(F32))).astype(BF16)
        for half in range(2):
            rows = rows_of(half, g)
            ko[rows, :] = out[half * size : (half + 1) * size, :]
            pltpu.make_async_copy(
                ko.at[rows, :], kv_out.at[rows, :], out_sem.at[2 * (len(GROUPS) + g) + half]
            ).start()

    z_start()
    wait(rot.at[pl.ds(0, (N - 1) * 16), :], r_recv)

    for i, (dy, dx) in enumerate(ORDER):
        matmul(dy, dx)
        if dx == 2:
            first_far(0, dy)
        if dy == 2:
            first_far(1, dx)
        for c in {6: (2,), 10: (1, 3), 14: (0,)}.get(i, ()):
            first_near(0, 0, c)
            first_near(1, 0, c)
    for i in range(3, 7):
        loads[i].wait()
    last = len(GROUPS) - 1
    squares = [None] * len(GROUPS)
    for g in range(last + 1):
        for c in CHUNKS:
            second(0, g, c)
            second(1, g, c)
            if g < last:
                first_near(0, g + 1, c)
                first_near(1, g + 1, c)
            if g == 1 and c == 2:
                z_finish()
            if g > 0 and c == 3:
                if g == 1:
                    wait(wkv.at[pl.ds(0, BLK // 2), :], sib_recv)
                project(g - 1, squares[g - 1])
        squares[g] = residual_rows(g)
    project(last, squares[last])
    for g in range(last + 1):
        finish(g)

    wait(att.at[pl.ds(0, N - 1)], a_send)
    wait(wkv.at[pl.ds(0, CK), pl.ds(0, (N - 1) * KVB)], k_send)
    wait(turned.at[pl.ds(0, N - 1)], r_send)
    wait(pb.at[pl.ds(0, 3)], p_send)
    wait(pb.at[0, pl.ds(0, 3)], q_send)
    wait(wkv.at[pl.ds(0, (PLANES - 1) * CK), :], z_send)
    wait(wkv.at[pl.ds(0, BLK // 2), :], sib_send)
    for g in range(last + 1):
        wait(kp[g].at[pl.ds(0, N - 1)], kv_send.at[g])
        for half in range(2):
            rows = rows_of(half, g)
            pltpu.make_async_copy(ro.at[rows, :], resid_out.at[rows, :], out_sem.at[2 * g + half]).wait()
            pltpu.make_async_copy(
                ko.at[rows, :], kv_out.at[rows, :], out_sem.at[2 * (len(GROUPS) + g) + half]
            ).wait()


def body(attn_out, head_signs, w_out, out_exp, residual, norm_gain, w_kv, kv_exp):
    vmem = pltpu.VMEM
    dma = pltpu.SemaphoreType.DMA
    groups = len(GROUPS)
    scratch = [
        pltpu.SMEM((N * LH,), jnp.int32),
        vmem((N, 16, BLK), BF16),
        vmem((N, 16, BLK), F32),
        vmem((N, 16, BLK), BF16),
        vmem((TOK, BLK), BF16),
        vmem((4, 4, BLK, BLK), BF16),
        vmem((4, 4, TOK, BLK), BF16),
        vmem((2, 4, 2, HALF, HCOL), BF16),
        vmem((2, 4, 2, HALF, BLK), BF16),
        vmem((2, 3, HALF, BLK), BF16),
        vmem((2, HALF, BLK), F32),
        vmem((2, 2, HALF, HCOL), BF16),
        vmem((2, 2, HALF, BLK), BF16),
        vmem((BLK, N * KVB), BF16),
        vmem((TOK, BLK), BF16),
        vmem((TOK, BLK), BF16),
        vmem((TOK, BLK), BF16),
        vmem((BLK,), BF16),
        vmem((1, BLK), jnp.int32),
        vmem((1, KVB), jnp.int32),
        vmem((TOK, KVB), BF16),
        [vmem((N, 2 * size + 16, KVB), BF16) for _, size in GROUPS],
        [vmem((N, 2 * size + 16, KVB), BF16) for _, size in GROUPS],
        dma((7,)),
        dma((16,)),
        dma((4 * groups,)),
        dma, dma, dma, dma, dma, dma,
        dma,
        dma((2, 4, 2)),
        dma((2, groups, 4, 2)),
        dma,
        dma((2, groups, 2)),
        dma((2, groups, 2)),
        dma, dma, dma, dma,
        dma((groups,)), dma((groups,)),
    ]
    anywhere = pl.BlockSpec(memory_space=pl.ANY)
    return pl.pallas_call(
        kernel,
        out_shape=(
            jax.ShapeDtypeStruct((TOK, BLK), BF16),
            jax.ShapeDtypeStruct((TOK, KVB), BF16),
        ),
        in_specs=[anywhere] * 8,
        out_specs=(anywhere, anywhere),
        scratch_shapes=scratch,
        compiler_params=pltpu.CompilerParams(
            collective_id=0, has_side_effects=True, vmem_limit_bytes=62 * 1024 * 1024
        ),
    )(
        attn_out, head_signs, w_out, out_exp.reshape(1, BLK), residual,
        norm_gain, w_kv, kv_exp.reshape(1, KVB),
    )


def solution(mesh):
    placed = (
        P("dp", "tensor"),
        P(),
        P("tensor", None),
        P("tensor"),
        P("dp", "tensor"),
        P("tensor"),
        P(None, "tensor"),
        P("tensor"),
    )
    return jax.shard_map(
        body,
        mesh=mesh,
        in_specs=placed,
        out_specs=(P("dp", "tensor"), P("dp", "tensor")),
        check_vma=False,
    )
```

time: 72.9 us -> 71 us (0.974)
  the two profiles are of different devices: /device:TPU:6 before, /device:TPU:480 now
where the time goes in v3:
time: 71 us; the launch traced here: 70.8 us
  Pallas kernels  67.1 us (95%)
  local copies, waits for them, and re-layouts  3.14 us (4%)
    pallas_call x1, Pallas kernels, body(): pl.pallas_call(kernel, out_shape=(jax.ShapeDtypeStruct((TOK, BLK), BF16),...  67.1 us
    unnamed x2, local copies, waits for them, and re-layouts  3.14 us

profile of v3, /device:TPU:480, one launch (start us, length us, event | category | flops | bytes accessed | tf_op | source)
XLA Modules:
  0.0 70.8 jit_solution(12670735266016399921)
XLA Ops:
  0.6 67.1 %shard_map.95 = (bf16[256,512]{1,0:T(8,128)(2,1)}, bf16[256,128]{1,0:T(8,128)(2,1)}) custom-call(bf16[256,512]{1,0:T(8,128)(2,1)} %attn.1, s32[64]{0:T(128)} %signs.1, bf16[512,8192]{1,0:T(8,128)(2,1)} %w_out.1, s32[1,512]{1,0:T(1,128)} %bitcast.2, bf16[256,512]{1,0:T(8,128)(2,1)} %residual.1, bf16[512]{0:T(512)(128)(2,1)} %gain.1, bf16[8192,128]{1,0:T(8,128)(2,1)} %w_kv.1, ...), custom_call_target="tpu_custom_call" | custom-call | tf_op jit(solution)/shard_map/pallas_call | solution.py:396
  67.7 1.7 %copy.12 = bf16[256,512]{1,0:T(8,128)(2,1)} copy(bf16[256,512]{1,0:T(8,128)(2,1)} %get-tuple-element.4) | data formatting | bytes 524288
  69.4 1.5 %copy.13 = bf16[256,128]{1,0:T(8,128)(2,1)} copy(bf16[256,128]{1,0:T(8,128)(2,1)} %get-tuple-element.5) | data formatting | bytes 131072

commit v4 on v3

--- a/solution.py
+++ b/solution.py
@@ -49,11 +49,11 @@
 def kernel(
     attn, signs, w_out, out_exp, residual, gain, w_kv, kv_exp,
     resid_out, kv_out,
-    sgn, att, mixed, turned, rot, w, pb, s1, f, q, own, s1b, fb,
+    sgn, att, mixed, turned, rot, w, pb, s1, f, q, own, fb,
     wkv, xn, res, ro, gn, oe, ke, ko, kp, kr,
     in_sem, w_sem, out_sem,
     a_send, a_recv, k_send, k_recv, r_send, r_recv,
-    p_send, s1_recv, f_recv, q_send, s1b_recv, fb_recv,
+    p_send, s1_recv, f_recv, q_send, fb_recv,
     z_send, z_recv, sib_send, sib_recv,
     kv_send, kv_recv,
 ):
@@ -61,8 +61,8 @@
     dp = lax.axis_index("dp")
     y, x = me // 4, lax.rem(me, 4)
     z, core = dp // 2, lax.rem(dp, 2)
-    plane = lax.rem(z, PLANES)
-    share = core * PLANES + plane
+    nz = lax.axis_size("dp") // 2
+    share = core * PLANES + lax.rem(z, PLANES)
 
     def at_yx(dy, dx):
         return lax.rem(y + dy, 4) * 4 + lax.rem(x + dx, 4)
@@ -71,9 +71,10 @@
         ({"tensor": at_yx(0, 1)}, {"tensor": at_yx(0, 3)}),
         ({"tensor": at_yx(1, 0)}, {"tensor": at_yx(3, 0)}),
     )
-    z_peers = [
-        {"dp": (z - plane + lax.rem(plane + k, PLANES)) * 2 + core} for k in range(1, PLANES)
-    ]
+
+    def at_z(k):
+        return {"dp": lax.rem(z + k + nz, nz) * 2 + core}
+
     sibling = {"dp": z * 2 + 1 - core}
 
     def send(src, dst, send_sem, recv_sem, to):
@@ -95,7 +96,7 @@
         pl.semaphore_signal(barrier, inc=1, device_id={"tensor": j}, device_id_type=MESH)
 
     to_peers(greet)
-    for to in (*z_peers, sibling):
+    for to in (at_z(1), at_z(-1), at_z(2), at_z(-2), sibling):
         pl.semaphore_signal(barrier, inc=1, device_id=to, device_id_type=MESH)
 
     mine = pl.ds(pl.multiple_of(me * 16, 16), 16)
@@ -121,7 +122,7 @@
         columns = pl.ds(pl.multiple_of(at_yx(dy, dx) * BLK, BLK), BLK)
         w_loads[dy, dx] = pltpu.make_async_copy(w_out.at[:, columns], w.at[dy, dx], w_sem.at[i])
 
-    pl.semaphore_wait(barrier, N - 1 + PLANES)
+    pl.semaphore_wait(barrier, N - 1 + 5)
 
     def send_tokens(j):
         rows = pl.ds(pl.multiple_of(j * 16, 16), 16)
@@ -162,8 +163,11 @@
         loads[2].wait()
         wait(wkv.at[pl.ds(0, CK), pl.ds(0, (N - 1) * KVB)], k_recv)
         part = wkv.at[my_rows, :]
-        for to in z_peers:
-            send(part, part, z_send, z_recv, to)
+        for k in (1, -1):
+            send(part, part, z_send, z_recv, at_z(k))
+        for i, k in enumerate((2, -2)):
+            rows = pl.ds(pl.multiple_of(share * CK + i * (CK // 2), CK // 2), CK // 2)
+            send(wkv.at[rows, :], wkv.at[rows, :], z_send, z_recv, at_z(k))
 
     def z_finish():
         wait(wkv.at[pl.ds(0, (PLANES - 1) * CK), :], z_recv)
@@ -216,25 +220,11 @@
         if c == 0:
             own[half, slot, :] = total
             return
-        if c == 2:
-            q[half, 1, slot, :] = total.astype(BF16)
-            for way in range(2):
-                send(
-                    q.at[half, 1, slot, pl.ds(way * HCOL, HCOL)], s1b.at[half, way, slot, :],
-                    q_send, s1b_recv.at[half, g, way], along[1 - half][way],
-                )
-            return
-        way = 0 if c == 1 else 1
-        part = slice(way * HCOL, (way + 1) * HCOL)
-        rest = slice((1 - way) * HCOL, (2 - way) * HCOL)
-        q[half, c - 1, slot, rest] = total[:, rest].astype(BF16)
-        wait(s1b.at[half, way, slot, :], s1b_recv.at[half, g, way])
-        q[half, c - 1, slot, part] = (
-            total[:, part] + s1b[half, way, slot, :].astype(F32)
-        ).astype(BF16)
+        q[half, c - 1, slot, :] = total.astype(BF16)
+        to = at_yx(c, 0) if half == 0 else at_yx(0, c)
         send(
-            q.at[half, c - 1, slot, :], fb.at[half, way, slot, :],
-            q_send, fb_recv.at[half, g, way], along[1 - half][way],
+            q.at[half, c - 1, slot, :], fb.at[half, c - 1, slot, :],
+            q_send, fb_recv.at[half, g, c - 1], {"tensor": to},
         )
 
     def residual_rows(g):
@@ -246,9 +236,9 @@
         for half in range(2):
             rows = rows_of(half, g)
             total = own[half, slot, :]
-            for way in range(2):
-                wait(fb.at[half, way, slot, :], fb_recv.at[half, g, way])
-                total = total + fb[half, way, slot, :].astype(F32)
+            for k in range(3):
+                wait(fb.at[half, k, slot, :], fb_recv.at[half, g, k])
+                total = total + fb[half, k, slot, :].astype(F32)
             out = (res[rows, :].astype(F32) + total * out_scale).astype(BF16)
             ro[rows, :] = out
             hidden = out.astype(F32)
@@ -316,20 +306,25 @@
         loads[i].wait()
     last = len(GROUPS) - 1
     squares = [None] * len(GROUPS)
+    for c in CHUNKS:
+        first_near(0, 1, c)
+        first_near(1, 1, c)
     for g in range(last + 1):
-        for c in CHUNKS:
+        for i, c in enumerate(CHUNKS):
             second(0, g, c)
             second(1, g, c)
-            if g < last:
-                first_near(0, g + 1, c)
-                first_near(1, g + 1, c)
-            if g == 1 and c == 2:
-                z_finish()
-            if g > 0 and c == 3:
+            if g + 2 <= last:
+                first_near(0, g + 2, c)
+                first_near(1, g + 2, c)
+            if g > 0 and i == 0:
+                squares[g - 1] = residual_rows(g - 1)
+                if g == 1:
+                    z_finish()
+            if g > 0 and i == 2:
                 if g == 1:
                     wait(wkv.at[pl.ds(0, BLK // 2), :], sib_recv)
                 project(g - 1, squares[g - 1])
-        squares[g] = residual_rows(g)
+    squares[last] = residual_rows(last)
     project(last, squares[last])
     for g in range(last + 1):
         finish(g)
@@ -367,8 +362,7 @@
         vmem((2, 4, 2, HALF, BLK), BF16),
         vmem((2, 3, HALF, BLK), BF16),
         vmem((2, HALF, BLK), F32),
-        vmem((2, 2, HALF, HCOL), BF16),
-        vmem((2, 2, HALF, BLK), BF16),
+        vmem((2, 3, HALF, BLK), BF16),
         vmem((BLK, N * KVB), BF16),
         vmem((TOK, BLK), BF16),
         vmem((TOK, BLK), BF16),
@@ -387,8 +381,7 @@
         dma((2, 4, 2)),
         dma((2, groups, 4, 2)),
         dma,
-        dma((2, groups, 2)),
-        dma((2, groups, 2)),
+        dma((2, groups, 3)),
         dma, dma, dma, dma,
         dma((groups,)), dma((groups,)),
     ]

time: 71 us -> 72.9 us (1.027)
  the two profiles are of different devices: /device:TPU:480 before, /device:TPU:1 now
where the time goes in v4:
time: 72.9 us; the launch traced here: 72.7 us
  Pallas kernels  68.9 us (95%)
  local copies, waits for them, and re-layouts  3.14 us (4%)
    pallas_call x1, Pallas kernels, body(): pl.pallas_call(kernel, out_shape=(jax.ShapeDtypeStruct((TOK, BLK), BF16),...  68.9 us
    unnamed x2, local copies, waits for them, and re-layouts  3.14 us

profile of v4, /device:TPU:1, one launch (start us, length us, event | category | flops | bytes accessed | tf_op | source)
XLA Modules:
  0.0 72.7 jit_solution(6413027296081794776)
XLA Ops:
  0.6 68.9 %shard_map.95 = (bf16[256,512]{1,0:T(8,128)(2,1)}, bf16[256,128]{1,0:T(8,128)(2,1)}) custom-call(bf16[256,512]{1,0:T(8,128)(2,1)} %attn.1, s32[64]{0:T(128)} %signs.1, bf16[512,8192]{1,0:T(8,128)(2,1)} %w_out.1, s32[1,512]{1,0:T(1,128)} %bitcast.2, bf16[256,512]{1,0:T(8,128)(2,1)} %residual.1, bf16[512]{0:T(512)(128)(2,1)} %gain.1, bf16[8192,128]{1,0:T(8,128)(2,1)} %w_kv.1, ...), custom_call_target="tpu_custom_call" | custom-call | tf_op jit(solution)/shard_map/pallas_call | solution.py:389
  69.5 1.7 %copy.12 = bf16[256,512]{1,0:T(8,128)(2,1)} copy(bf16[256,512]{1,0:T(8,128)(2,1)} %get-tuple-element.4) | data formatting | bytes 524288
  71.2 1.5 %copy.13 = bf16[256,128]{1,0:T(8,128)(2,1)} copy(bf16[256,128]{1,0:T(8,128)(2,1)} %get-tuple-element.5) | data formatting | bytes 131072

commit v5 on v4

--- a/solution.py
+++ b/solution.py
@@ -17,7 +17,7 @@
 KVB = 128
 HALF = TOK // 2
 HCOL = BLK // 2
-GROUPS = ((0, 64), (64, 32), (96, 32))
+HROW = HALF // 2
 LANES = 128
 PLANES = 4
 SHARES = 2 * PLANES
@@ -49,13 +49,14 @@
 def kernel(
     attn, signs, w_out, out_exp, residual, gain, w_kv, kv_exp,
     resid_out, kv_out,
-    sgn, att, mixed, turned, rot, w, pb, s1, f, q, own, fb,
-    wkv, xn, res, ro, gn, oe, ke, ko, kp, kr,
+    sgn, att, mixed, turned, rot, w, pb, s1, f, q, own, tot, s1b, fb,
+    wkv, xn, res, ro, gn, oe, ke, ko, sqs, sqr,
+    pk, ks1, kf, kq, kown, ktot, ks1b, kfb,
     in_sem, w_sem, out_sem,
     a_send, a_recv, k_send, k_recv, r_send, r_recv,
-    p_send, s1_recv, f_recv, q_send, fb_recv,
+    p_send, s1_recv, f_recv, q_send, s1b_recv, fb_recv,
     z_send, z_recv, sib_send, sib_recv,
-    kv_send, kv_recv,
+    sq_send, sq_recv, pk_send, ks1_recv, kf_recv, kq_send, ks1b_recv, kfb_recv,
 ):
     me = lax.axis_index("tensor")
     dp = lax.axis_index("dp")
@@ -177,9 +178,8 @@
     def block(half, c, a):
         return (c, a) if half == 0 else (a, c)
 
-    def rows_of(half, g):
-        start, size = GROUPS[g]
-        return pl.ds(half * HALF + start, size)
+    def rows_of(half):
+        return pl.ds(half * HALF, HALF)
 
     def matmul(dy, dx):
         w_loads[dy, dx].wait()
@@ -193,102 +193,158 @@
                 s1.at[half, c, way], p_send, s1_recv.at[half, c, way], along[half][way],
             )
 
-    def first_near(half, g, c):
-        start, size = GROUPS[g]
-        slot, rows = pl.ds(start, size), rows_of(half, g)
+    def first_near(half, c):
+        rows = rows_of(half)
         for way, a in enumerate((1, 3)):
             dy, dx = block(half, c, a)
             part = pl.ds(way * HCOL, HCOL)
-            if g == 0:
-                wait(s1.at[half, c, way], s1_recv.at[half, c, way])
+            wait(s1.at[half, c, way], s1_recv.at[half, c, way])
             pb[dy, dx, rows, part] = (
-                pb[dy, dx, rows, part].astype(F32) + s1[half, c, way, slot, :].astype(F32)
+                pb[dy, dx, rows, part].astype(F32) + s1[half, c, way].astype(F32)
             ).astype(BF16)
             send(
-                pb.at[dy, dx, rows, :], f.at[half, c, way, slot, :],
-                p_send, f_recv.at[half, g, c, way], along[half][way],
-            )
-
-    def second(half, g, c):
-        start, size = GROUPS[g]
-        slot, rows = pl.ds(start, size), rows_of(half, g)
+                pb.at[dy, dx, rows, :], f.at[half, c, way],
+                p_send, f_recv.at[half, c, way], along[half][way],
+            )
+
+    def second(half, c):
         dy, dx = block(half, c, 0)
-        total = pb[dy, dx, rows, :].astype(F32)
-        for way in range(2):
-            wait(f.at[half, c, way, slot, :], f_recv.at[half, g, c, way])
-            total = total + f[half, c, way, slot, :].astype(F32)
+        total = pb[dy, dx, rows_of(half), :].astype(F32)
+        for way in range(2):
+            wait(f.at[half, c, way], f_recv.at[half, c, way])
+            total = total + f[half, c, way].astype(F32)
         if c == 0:
-            own[half, slot, :] = total
+            own[half] = total
             return
-        q[half, c - 1, slot, :] = total.astype(BF16)
-        to = at_yx(c, 0) if half == 0 else at_yx(0, c)
-        send(
-            q.at[half, c - 1, slot, :], fb.at[half, c - 1, slot, :],
-            q_send, fb_recv.at[half, g, c - 1], {"tensor": to},
-        )
-
-    def residual_rows(g):
-        start, size = GROUPS[g]
-        slot = pl.ds(start, size)
-        out_scale = jnp.exp2(oe[...].astype(F32))
-        gains = gn[...].astype(F32).reshape(1, BLK)
-        squares = []
-        for half in range(2):
-            rows = rows_of(half, g)
-            total = own[half, slot, :]
-            for k in range(3):
-                wait(fb.at[half, k, slot, :], fb_recv.at[half, g, k])
-                total = total + fb[half, k, slot, :].astype(F32)
-            out = (res[rows, :].astype(F32) + total * out_scale).astype(BF16)
-            ro[rows, :] = out
-            hidden = out.astype(F32)
-            xn[pl.ds(2 * start + half * size, size), :] = (hidden * gains).astype(BF16)
-            squares.append(jnp.sum(hidden * hidden, axis=1, keepdims=True))
-            pltpu.make_async_copy(ro.at[rows, :], resid_out.at[rows, :], out_sem.at[2 * g + half]).start()
-        if 2 * size < LANES:
-            squares.append(jnp.zeros((LANES - 2 * size, 1), F32))
-        column = jnp.concatenate(squares, axis=0)
-        row = jnp.transpose(jnp.broadcast_to(column, (LANES, LANES)))[:16, :]
-        high = row.astype(BF16).astype(F32)
-        mid = (row - high).astype(BF16).astype(F32)
-        low = row - high - mid
-        index = lax.broadcasted_iota(jnp.int32, (16, LANES), 0)
-        return jnp.where(index == 0, high, jnp.where(index == 1, mid, jnp.where(index == 2, low, 0.0)))
-
-    def project(g, squares):
-        start, size = GROUPS[g]
-        squares = squares.astype(BF16)
-        hidden = xn[pl.ds(2 * start, 2 * size), :]
-        for i in CHUNKS:
-            yy = lax.rem(y + i, 4)
-            columns = pl.ds(pl.multiple_of(yy * 4 * KVB, 4 * KVB), 4 * KVB)
-            part = jnp.dot(hidden, wkv[:, columns], preferred_element_type=F32).astype(BF16)
-            for k in range(4):
-                kp[g][yy * 4 + k, : 2 * size, :] = part[:, k * KVB : (k + 1) * KVB]
-                kp[g][yy * 4 + k, 2 * size :, :] = squares
-            for k in CHUNKS:
-                if i or k:
-                    j = at_yx(i, k)
-                    send(kp[g].at[j], kr[g].at[me], kv_send.at[g], kv_recv.at[g], {"tensor": j})
-        kr[g][me] = kp[g][me]
-
-    def finish(g):
-        start, size = GROUPS[g]
-        wait(kr[g].at[pl.ds(0, N - 1)], kv_recv.at[g])
-        total = kr[g][0].astype(F32)
+        if c == 2:
+            q[half, 1] = total.astype(BF16)
+            for way in range(2):
+                send(
+                    q.at[half, 1, :, pl.ds(way * HCOL, HCOL)], s1b.at[half, way],
+                    q_send, s1b_recv.at[half, way], along[1 - half][way],
+                )
+            return
+        way = 0 if c == 1 else 1
+        rest = slice((1 - way) * HCOL, (2 - way) * HCOL)
+        tot[half, way] = total[:, way * HCOL : (way + 1) * HCOL]
+        q[half, c - 1, :, rest] = total[:, rest].astype(BF16)
+
+    def second_near(half):
+        for way, c in enumerate((1, 3)):
+            wait(s1b.at[half, way], s1b_recv.at[half, way])
+            q[half, c - 1, :, way * HCOL : (way + 1) * HCOL] = (
+                tot[half, way] + s1b[half, way].astype(F32)
+            ).astype(BF16)
+            send(
+                q.at[half, c - 1], fb.at[half, way],
+                q_send, fb_recv.at[half, way], along[1 - half][way],
+            )
+
+    def residual_rows(half):
+        rows = rows_of(half)
+        total = own[half]
+        for way in range(2):
+            wait(fb.at[half, way], fb_recv.at[half, way])
+            total = total + fb[half, way].astype(F32)
+        out = (res[rows, :].astype(F32) + total * jnp.exp2(oe[...].astype(F32))).astype(BF16)
+        ro[rows, :] = out
+        pltpu.make_async_copy(ro.at[rows, :], resid_out.at[rows, :], out_sem.at[half]).start()
+        hidden = out.astype(F32)
+        xn[rows, :] = (hidden * gn[...].astype(F32).reshape(1, BLK)).astype(BF16)
+        column = jnp.sum(hidden * hidden, axis=1, keepdims=True)
+        return jnp.transpose(jnp.broadcast_to(column, (HALF, LANES)))[:8, :]
+
+    def send_squares(first_half, second_half):
+        index = lax.broadcasted_iota(jnp.int32, (8, LANES), 0)
+        sqs[...] = jnp.where(index == 0, first_half, second_half)
+        sqr[me] = sqs[...]
+
+        def send_square(j):
+            send(sqs, sqr.at[me], sq_send, sq_recv, {"tensor": j})
+
+        to_peers(send_square)
+
+    def product(dy):
+        yy = lax.rem(y + dy, 4)
+        columns = pl.ds(pl.multiple_of(yy * 4 * KVB, 4 * KVB), 4 * KVB)
+        part = jnp.dot(xn[...], wkv[:, columns], preferred_element_type=F32).astype(BF16)
+        for k in range(4):
+            pk[dy, lax.rem(k + 4 - x, 4)] = part[:, k * KVB : (k + 1) * KVB]
+
+    def kv_first_far(half, c):
+        dy, dx = block(half, c, 2)
+        for way in range(2):
+            send(
+                pk.at[dy, dx, pl.ds(half * HALF + way * HROW, HROW), :], ks1.at[half, c, way],
+                pk_send, ks1_recv.at[half, c, way], along[half][way],
+            )
+
+    def kv_first_near(half, c):
+        for way, a in enumerate((1, 3)):
+            dy, dx = block(half, c, a)
+            part = pl.ds(half * HALF + way * HROW, HROW)
+            wait(ks1.at[half, c, way], ks1_recv.at[half, c, way])
+            pk[dy, dx, part, :] = (
+                pk[dy, dx, part, :].astype(F32) + ks1[half, c, way].astype(F32)
+            ).astype(BF16)
+            send(
+                pk.at[dy, dx, rows_of(half), :], kf.at[half, c, way],
+                pk_send, kf_recv.at[half, c, way], along[half][way],
+            )
+
+    def kv_second(half, c):
+        dy, dx = block(half, c, 0)
+        total = pk[dy, dx, rows_of(half), :].astype(F32)
+        for way in range(2):
+            wait(kf.at[half, c, way], kf_recv.at[half, c, way])
+            total = total + kf[half, c, way].astype(F32)
+        if c == 0:
+            kown[half] = total
+            return
+        if c == 2:
+            kq[half, 1] = total.astype(BF16)
+            for way in range(2):
+                send(
+                    kq.at[half, 1, pl.ds(way * HROW, HROW), :], ks1b.at[half, way],
+                    kq_send, ks1b_recv.at[half, way], along[1 - half][way],
+                )
+            return
+        way = 0 if c == 1 else 1
+        rest = slice((1 - way) * HROW, (2 - way) * HROW)
+        ktot[half, way] = total[way * HROW : (way + 1) * HROW, :]
+        kq[half, c - 1, rest, :] = total[rest, :].astype(BF16)
+
+    def kv_second_near(half):
+        for way, c in enumerate((1, 3)):
+            wait(ks1b.at[half, way], ks1b_recv.at[half, way])
+            kq[half, c - 1, way * HROW : (way + 1) * HROW, :] = (
+                ktot[half, way] + ks1b[half, way].astype(F32)
+            ).astype(BF16)
+            send(
+                kq.at[half, c - 1], kfb.at[half, way],
+                kq_send, kfb_recv.at[half, way], along[1 - half][way],
+            )
+
+    def row_scales():
+        wait(sqr.at[pl.ds(0, N - 1)], sq_recv)
+        total_sq = sqr[0]
         for s in range(1, N):
-            total = total + kr[g][s].astype(F32)
-        at = 2 * size
-        total_sq = total[at : at + 1, :] + total[at + 1 : at + 2, :] + total[at + 2 : at + 3, :]
+            total_sq = total_sq + sqr[s]
         inv = lax.rsqrt(total_sq / D + 1e-05)
-        scale = jnp.transpose(jnp.broadcast_to(inv, (LANES, LANES)))[:at, :]
-        out = (total[:at, :] * scale * jnp.exp2(ke[...].astype(F32))).astype(BF16)
-        for half in range(2):
-            rows = rows_of(half, g)
-            ko[rows, :] = out[half * size : (half + 1) * size, :]
-            pltpu.make_async_copy(
-                ko.at[rows, :], kv_out.at[rows, :], out_sem.at[2 * (len(GROUPS) + g) + half]
-            ).start()
+        return [
+            jnp.transpose(jnp.broadcast_to(inv[half : half + 1, :], (LANES, HALF)))
+            * jnp.exp2(ke[...].astype(F32))
+            for half in range(2)
+        ]
+
+    def finish(half, scale):
+        total = kown[half]
+        for way in range(2):
+            wait(kfb.at[half, way], kfb_recv.at[half, way])
+            total = total + kfb[half, way].astype(F32)
+        rows = rows_of(half)
+        ko[rows, :] = (total * scale).astype(BF16)
+        pltpu.make_async_copy(ko.at[rows, :], kv_out.at[rows, :], out_sem.at[2 + half]).start()
 
     z_start()
     wait(rot.at[pl.ds(0, (N - 1) * 16), :], r_recv)
@@ -300,34 +356,37 @@
         if dy == 2:
             first_far(1, dx)
         for c in {6: (2,), 10: (1, 3), 14: (0,)}.get(i, ()):
-            first_near(0, 0, c)
-            first_near(1, 0, c)
+            first_near(0, c)
+            first_near(1, c)
     for i in range(3, 7):
         loads[i].wait()
-    last = len(GROUPS) - 1
-    squares = [None] * len(GROUPS)
     for c in CHUNKS:
-        first_near(0, 1, c)
-        first_near(1, 1, c)
-    for g in range(last + 1):
-        for i, c in enumerate(CHUNKS):
-            second(0, g, c)
-            second(1, g, c)
-            if g + 2 <= last:
-                first_near(0, g + 2, c)
-                first_near(1, g + 2, c)
-            if g > 0 and i == 0:
-                squares[g - 1] = residual_rows(g - 1)
-                if g == 1:
-                    z_finish()
-            if g > 0 and i == 2:
-                if g == 1:
-                    wait(wkv.at[pl.ds(0, BLK // 2), :], sib_recv)
-                project(g - 1, squares[g - 1])
-    squares[last] = residual_rows(last)
-    project(last, squares[last])
-    for g in range(last + 1):
-        finish(g)
+        second(0, c)
+        second(1, c)
+        if c == 1:
+            z_finish()
+    second_near(0)
+    second_near(1)
+    squares = [residual_rows(0), residual_rows(1)]
+    send_squares(*squares)
+    wait(wkv.at[pl.ds(0, BLK // 2), :], sib_recv)
+    for c in CHUNKS:
+        product(c)
+        kv_first_far(0, c)
+        if c == 2:
+            for a in CHUNKS:
+                kv_first_far(1, a)
+    for c in CHUNKS:
+        kv_first_near(0, c)
+        kv_first_near(1, c)
+    scales = row_scales()
+    for c in CHUNKS:
+        kv_second(0, c)
+        kv_second(1, c)
+    kv_second_near(0)
+    kv_second_near(1)
+    finish(0, scales[0])
+    finish(1, scales[1])
 
     wait(att.at[pl.ds(0, N - 1)], a_send)
     wait(wkv.at[pl.ds(0, CK), pl.ds(0, (N - 1) * KVB)], k_send)
@@ -336,20 +395,18 @@
     wait(pb.at[0, pl.ds(0, 3)], q_send)
     wait(wkv.at[pl.ds(0, (PLANES - 1) * CK), :], z_send)
     wait(wkv.at[pl.ds(0, BLK // 2), :], sib_send)
-    for g in range(last + 1):
-        wait(kp[g].at[pl.ds(0, N - 1)], kv_send.at[g])
-        for half in range(2):
-            rows = rows_of(half, g)
-            pltpu.make_async_copy(ro.at[rows, :], resid_out.at[rows, :], out_sem.at[2 * g + half]).wait()
-            pltpu.make_async_copy(
-                ko.at[rows, :], kv_out.at[rows, :], out_sem.at[2 * (len(GROUPS) + g) + half]
-            ).wait()
+    wait(sqr.at[pl.ds(0, N - 1)], sq_send)
+    wait(pk.at[pl.ds(0, 3)], pk_send)
+    wait(pk.at[0, pl.ds(0, 3)], kq_send)
+    for half in range(2):
+        rows = rows_of(half)
+        pltpu.make_async_copy(ro.at[rows, :], resid_out.at[rows, :], out_sem.at[half]).wait()
+        pltpu.make_async_copy(ko.at[rows, :], kv_out.at[rows, :], out_sem.at[2 + half]).wait()
 
 
 def body(attn_out, head_signs, w_out, out_exp, residual, norm_gain, w_kv, kv_exp):
     vmem = pltpu.VMEM
     dma = pltpu.SemaphoreType.DMA
-    groups = len(GROUPS)
     scratch = [
         pltpu.SMEM((N * LH,), jnp.int32),
         vmem((N, 16, BLK), BF16),
@@ -362,7 +419,9 @@
         vmem((2, 4, 2, HALF, BLK), BF16),
         vmem((2, 3, HALF, BLK), BF16),
         vmem((2, HALF, BLK), F32),
-        vmem((2, 3, HALF, BLK), BF16),
+        vmem((2, 2, HALF, HCOL), F32),
+        vmem((2, 2, HALF, HCOL), BF16),
+        vmem((2, 2, HALF, BLK), BF16),
         vmem((BLK, N * KVB), BF16),
         vmem((TOK, BLK), BF16),
         vmem((TOK, BLK), BF16),
@@ -371,19 +430,34 @@
         vmem((1, BLK), jnp.int32),
         vmem((1, KVB), jnp.int32),
         vmem((TOK, KVB), BF16),
-        [vmem((N, 2 * size + 16, KVB), BF16) for _, size in GROUPS],
-        [vmem((N, 2 * size + 16, KVB), BF16) for _, size in GROUPS],
+        vmem((8, LANES), F32),
+        vmem((N, 8, LANES), F32),
+        vmem((4, 4, TOK, KVB), BF16),
+        vmem((2, 4, 2, HROW, KVB), BF16),
+        vmem((2, 4, 2, HALF, KVB), BF16),
+        vmem((2, 3, HALF, KVB), BF16),
+        vmem((2, HALF, KVB), F32),
+        vmem((2, 2, HROW, KVB), F32),
+        vmem((2, 2, HROW, KVB), BF16),
+        vmem((2, 2, HALF, KVB), BF16),
         dma((7,)),
         dma((16,)),
-        dma((4 * groups,)),
+        dma((4,)),
         dma, dma, dma, dma, dma, dma,
         dma,
         dma((2, 4, 2)),
-        dma((2, groups, 4, 2)),
+        dma((2, 4, 2)),
         dma,
-        dma((2, groups, 3)),
+        dma((2, 2)),
+        dma((2, 2)),
         dma, dma, dma, dma,
-        dma((groups,)), dma((groups,)),
+        dma, dma,
+        dma,
+        dma((2, 4, 2)),
+        dma((2, 4, 2)),
+        dma,
+        dma((2, 2)),
+        dma((2, 2)),
     ]
     anywhere = pl.BlockSpec(memory_space=pl.ANY)
     return pl.pallas_call(

time: 72.9 us -> 70 us (0.960)
  the two profiles are of different devices: /device:TPU:1 before, /device:TPU:6 now
where the time goes in v5:
time: 70 us; the launch traced here: 69.1 us
  Pallas kernels  65.3 us (93%)
  local copies, waits for them, and re-layouts  3.14 us (4%)
    pallas_call x1, Pallas kernels, body(): pl.pallas_call(kernel, out_shape=(jax.ShapeDtypeStruct((TOK, BLK), BF16),...  65.3 us
    unnamed x2, local copies, waits for them, and re-layouts  3.14 us

profile of v5, /device:TPU:6, one launch (start us, length us, event | category | flops | bytes accessed | tf_op | source)
XLA Modules:
  0.0 69.1 jit_solution(11686353975954653457)
XLA Ops:
  0.6 65.3 %shard_map.95 = (bf16[256,512]{1,0:T(8,128)(2,1)}, bf16[256,128]{1,0:T(8,128)(2,1)}) custom-call(bf16[256,512]{1,0:T(8,128)(2,1)} %attn.1, s32[64]{0:T(128)} %signs.1, bf16[512,8192]{1,0:T(8,128)(2,1)} %w_out.1, s32[1,512]{1,0:T(1,128)} %bitcast.2, bf16[256,512]{1,0:T(8,128)(2,1)} %residual.1, bf16[512]{0:T(512)(128)(2,1)} %gain.1, bf16[8192,128]{1,0:T(8,128)(2,1)} %w_kv.1, ...), custom_call_target="tpu_custom_call" | custom-call | tf_op jit(solution)/shard_map/pallas_call | solution.py:463
  66.0 1.7 %copy.12 = bf16[256,512]{1,0:T(8,128)(2,1)} copy(bf16[256,512]{1,0:T(8,128)(2,1)} %get-tuple-element.4) | data formatting | bytes 524288
  67.7 1.5 %copy.13 = bf16[256,128]{1,0:T(8,128)(2,1)} copy(bf16[256,128]{1,0:T(8,128)(2,1)} %get-tuple-element.5) | data formatting | bytes 131072

commit v6 on v5

--- a/solution.py
+++ b/solution.py
@@ -17,7 +17,6 @@
 KVB = 128
 HALF = TOK // 2
 HCOL = BLK // 2
-HROW = HALF // 2
 LANES = 128
 PLANES = 4
 SHARES = 2 * PLANES
@@ -49,14 +48,14 @@
 def kernel(
     attn, signs, w_out, out_exp, residual, gain, w_kv, kv_exp,
     resid_out, kv_out,
-    sgn, att, mixed, turned, rot, w, pb, s1, f, q, own, tot, s1b, fb,
+    sgn, att, mixed, turned, rot, w, pb, s1, f, q, own, s1b, fb,
     wkv, xn, res, ro, gn, oe, ke, ko, sqs, sqr,
-    pk, ks1, kf, kq, kown, ktot, ks1b, kfb,
+    pk, kf, kq, kown, kfb,
     in_sem, w_sem, out_sem,
     a_send, a_recv, k_send, k_recv, r_send, r_recv,
     p_send, s1_recv, f_recv, q_send, s1b_recv, fb_recv,
     z_send, z_recv, sib_send, sib_recv,
-    sq_send, sq_recv, pk_send, ks1_recv, kf_recv, kq_send, ks1b_recv, kfb_recv,
+    sq_send, sq_recv, pk_send, kf_recv, kq_send, kfb_recv,
 ):
     me = lax.axis_index("tensor")
     dp = lax.axis_index("dp")
@@ -76,6 +75,18 @@
     def at_z(k):
         return {"dp": lax.rem(z + k + nz, nz) * 2 + core}
 
+    top = nz - 1
+    z_peers = (
+        (z < top, 1), (z > 0, -1), (z < top - 1, 2), (z > 1, -2),
+        ((z == 0) | (z == top - 3), 3), ((z == 3) | (z == top), -3),
+    )
+    z_sends = (
+        (z < top, 1, 0, CK), (z > 0, -1, 0, CK),
+        (z < top - 1, 2, 0, CK // 2), ((z < top - 1) & (z >= top - 3), 2, CK // 2, CK // 2),
+        (z > 1, -2, CK // 2, CK // 2), ((z > 1) & (z <= 3), -2, 0, CK // 2),
+        (z == top - 3, 3, 0, CK), (z == 3, -3, 0, CK),
+    )
+
     sibling = {"dp": z * 2 + 1 - core}
 
     def send(src, dst, send_sem, recv_sem, to):
@@ -97,8 +108,13 @@
         pl.semaphore_signal(barrier, inc=1, device_id={"tensor": j}, device_id_type=MESH)
 
     to_peers(greet)
-    for to in (at_z(1), at_z(-1), at_z(2), at_z(-2), sibling):
-        pl.semaphore_signal(barrier, inc=1, device_id=to, device_id_type=MESH)
+    pl.semaphore_signal(barrier, inc=1, device_id=sibling, device_id_type=MESH)
+    for there, k in z_peers:
+
+        @pl.when(there)
+        def _(k=k):
+            pl.semaphore_signal(barrier, inc=1, device_id=at_z(k), device_id_type=MESH)
+
 
     mine = pl.ds(pl.multiple_of(me * 16, 16), 16)
     my_rows = pl.ds(pl.multiple_of(share * CK, CK), CK)
@@ -123,7 +139,7 @@
         columns = pl.ds(pl.multiple_of(at_yx(dy, dx) * BLK, BLK), BLK)
         w_loads[dy, dx] = pltpu.make_async_copy(w_out.at[:, columns], w.at[dy, dx], w_sem.at[i])
 
-    pl.semaphore_wait(barrier, N - 1 + 5)
+    pl.semaphore_wait(barrier, N + sum(there.astype(jnp.int32) for there, _ in z_peers))
 
     def send_tokens(j):
         rows = pl.ds(pl.multiple_of(j * 16, 16), 16)
@@ -163,12 +179,12 @@
     def z_start():
         loads[2].wait()
         wait(wkv.at[pl.ds(0, CK), pl.ds(0, (N - 1) * KVB)], k_recv)
-        part = wkv.at[my_rows, :]
-        for k in (1, -1):
-            send(part, part, z_send, z_recv, at_z(k))
-        for i, k in enumerate((2, -2)):
-            rows = pl.ds(pl.multiple_of(share * CK + i * (CK // 2), CK // 2), CK // 2)
-            send(wkv.at[rows, :], wkv.at[rows, :], z_send, z_recv, at_z(k))
+        for there, k, low, count in z_sends:
+
+            @pl.when(there)
+            def _(k=k, low=low, count=count):
+                rows = pl.ds(pl.multiple_of(share * CK + low, CK // 2), count)
+                send(wkv.at[rows, :], wkv.at[rows, :], z_send, z_recv, at_z(k))
 
     def z_finish():
         wait(wkv.at[pl.ds(0, (PLANES - 1) * CK), :], z_recv)
@@ -225,20 +241,15 @@
                 )
             return
         way = 0 if c == 1 else 1
+        part = slice(way * HCOL, (way + 1) * HCOL)
         rest = slice((1 - way) * HCOL, (2 - way) * HCOL)
-        tot[half, way] = total[:, way * HCOL : (way + 1) * HCOL]
         q[half, c - 1, :, rest] = total[:, rest].astype(BF16)
-
-    def second_near(half):
-        for way, c in enumerate((1, 3)):
-            wait(s1b.at[half, way], s1b_recv.at[half, way])
-            q[half, c - 1, :, way * HCOL : (way + 1) * HCOL] = (
-                tot[half, way] + s1b[half, way].astype(F32)
-            ).astype(BF16)
-            send(
-                q.at[half, c - 1], fb.at[half, way],
-                q_send, fb_recv.at[half, way], along[1 - half][way],
-            )
+        wait(s1b.at[half, way], s1b_recv.at[half, way])
+        q[half, c - 1, :, part] = (total[:, part] + s1b[half, way].astype(F32)).astype(BF16)
+        send(
+            q.at[half, c - 1], fb.at[half, way],
+            q_send, fb_recv.at[half, way], along[1 - half][way],
+        )
 
     def residual_rows(half):
         rows = rows_of(half)
@@ -271,59 +282,30 @@
         for k in range(4):
             pk[dy, lax.rem(k + 4 - x, 4)] = part[:, k * KVB : (k + 1) * KVB]
 
-    def kv_first_far(half, c):
-        dy, dx = block(half, c, 2)
-        for way in range(2):
+    def kv_first(half, c):
+        for a in (2, 1, 3):
+            dy, dx = block(half, c, a)
+            to = at_yx(0, a) if half == 0 else at_yx(a, 0)
             send(
-                pk.at[dy, dx, pl.ds(half * HALF + way * HROW, HROW), :], ks1.at[half, c, way],
-                pk_send, ks1_recv.at[half, c, way], along[half][way],
-            )
-
-    def kv_first_near(half, c):
-        for way, a in enumerate((1, 3)):
-            dy, dx = block(half, c, a)
-            part = pl.ds(half * HALF + way * HROW, HROW)
-            wait(ks1.at[half, c, way], ks1_recv.at[half, c, way])
-            pk[dy, dx, part, :] = (
-                pk[dy, dx, part, :].astype(F32) + ks1[half, c, way].astype(F32)
-            ).astype(BF16)
-            send(
-                pk.at[dy, dx, rows_of(half), :], kf.at[half, c, way],
-                pk_send, kf_recv.at[half, c, way], along[half][way],
+                pk.at[dy, dx, rows_of(half), :], kf.at[half, c, a - 1],
+                pk_send, kf_recv.at[half, c, a - 1], {"tensor": to},
             )
 
     def kv_second(half, c):
         dy, dx = block(half, c, 0)
         total = pk[dy, dx, rows_of(half), :].astype(F32)
-        for way in range(2):
-            wait(kf.at[half, c, way], kf_recv.at[half, c, way])
-            total = total + kf[half, c, way].astype(F32)
+        for k in range(3):
+            wait(kf.at[half, c, k], kf_recv.at[half, c, k])
+            total = total + kf[half, c, k].astype(F32)
         if c == 0:
             kown[half] = total
             return
-        if c == 2:
-            kq[half, 1] = total.astype(BF16)
-            for way in range(2):
-                send(
-                    kq.at[half, 1, pl.ds(way * HROW, HROW), :], ks1b.at[half, way],
-                    kq_send, ks1b_recv.at[half, way], along[1 - half][way],
-                )
-            return
-        way = 0 if c == 1 else 1
-        rest = slice((1 - way) * HROW, (2 - way) * HROW)
-        ktot[half, way] = total[way * HROW : (way + 1) * HROW, :]
-        kq[half, c - 1, rest, :] = total[rest, :].astype(BF16)
-
-    def kv_second_near(half):
-        for way, c in enumerate((1, 3)):
-            wait(ks1b.at[half, way], ks1b_recv.at[half, way])
-            kq[half, c - 1, way * HROW : (way + 1) * HROW, :] = (
-                ktot[half, way] + ks1b[half, way].astype(F32)
-            ).astype(BF16)
-            send(
-                kq.at[half, c - 1], kfb.at[half, way],
-                kq_send, kfb_recv.at[half, way], along[1 - half][way],
-            )
+        kq[half, c - 1] = total.astype(BF16)
+        to = at_yx(c, 0) if half == 0 else at_yx(0, c)
+        send(
+            kq.at[half, c - 1], kfb.at[half, c - 1],
+            kq_send, kfb_recv.at[half, c - 1], {"tensor": to},
+        )
 
     def row_scales():
         wait(sqr.at[pl.ds(0, N - 1)], sq_recv)
@@ -339,9 +321,9 @@
 
     def finish(half, scale):
         total = kown[half]
-        for way in range(2):
-            wait(kfb.at[half, way], kfb_recv.at[half, way])
-            total = total + kfb[half, way].astype(F32)
+        for k in range(3):
+            wait(kfb.at[half, k], kfb_recv.at[half, k])
+            total = total + kfb[half, k].astype(F32)
         rows = rows_of(half)
         ko[rows, :] = (total * scale).astype(BF16)
         pltpu.make_async_copy(ko.at[rows, :], kv_out.at[rows, :], out_sem.at[2 + half]).start()
@@ -365,26 +347,20 @@
         second(1, c)
         if c == 1:
             z_finish()
-    second_near(0)
-    second_near(1)
     squares = [residual_rows(0), residual_rows(1)]
     send_squares(*squares)
     wait(wkv.at[pl.ds(0, BLK // 2), :], sib_recv)
     for c in CHUNKS:
         product(c)
-        kv_first_far(0, c)
-        if c == 2:
-            for a in CHUNKS:
-                kv_first_far(1, a)
+        kv_first(0, c)
+        if c == 3:
+            for k in CHUNKS:
+                kv_first(1, k)
     for c in CHUNKS:
-        kv_first_near(0, c)
-        kv_first_near(1, c)
-    scales = row_scales()
-    for c in CHUNKS:
+        if c == 0:
+            scales = row_scales()
         kv_second(0, c)
         kv_second(1, c)
-    kv_second_near(0)
-    kv_second_near(1)
     finish(0, scales[0])
     finish(1, scales[1])
 
@@ -393,7 +369,12 @@
     wait(turned.at[pl.ds(0, N - 1)], r_send)
     wait(pb.at[pl.ds(0, 3)], p_send)
     wait(pb.at[0, pl.ds(0, 3)], q_send)
-    wait(wkv.at[pl.ds(0, (PLANES - 1) * CK), :], z_send)
+    for there, _, _, count in z_sends:
+
+        @pl.when(there)
+        def _(count=count):
+            wait(wkv.at[pl.ds(0, count), :], z_send)
+
     wait(wkv.at[pl.ds(0, BLK // 2), :], sib_send)
     wait(sqr.at[pl.ds(0, N - 1)], sq_send)
     wait(pk.at[pl.ds(0, 3)], pk_send)
@@ -419,7 +400,6 @@
         vmem((2, 4, 2, HALF, BLK), BF16),
         vmem((2, 3, HALF, BLK), BF16),
         vmem((2, HALF, BLK), F32),
-        vmem((2, 2, HALF, HCOL), F32),
         vmem((2, 2, HALF, HCOL), BF16),
         vmem((2, 2, HALF, BLK), BF16),
         vmem((BLK, N * KVB), BF16),
@@ -433,13 +413,10 @@
         vmem((8, LANES), F32),
         vmem((N, 8, LANES), F32),
         vmem((4, 4, TOK, KVB), BF16),
-        vmem((2, 4, 2, HROW, KVB), BF16),
-        vmem((2, 4, 2, HALF, KVB), BF16),
+        vmem((2, 4, 3, HALF, KVB), BF16),
         vmem((2, 3, HALF, KVB), BF16),
         vmem((2, HALF, KVB), F32),
-        vmem((2, 2, HROW, KVB), F32),
-        vmem((2, 2, HROW, KVB), BF16),
-        vmem((2, 2, HALF, KVB), BF16),
+        vmem((2, 3, HALF, KVB), BF16),
         dma((7,)),
         dma((16,)),
         dma((4,)),
@@ -453,11 +430,9 @@
         dma, dma, dma, dma,
         dma, dma,
         dma,
-        dma((2, 4, 2)),
-        dma((2, 4, 2)),
+        dma((2, 4, 3)),
         dma,
-        dma((2, 2)),
-        dma((2, 2)),
+        dma((2, 3)),
     ]
     anywhere = pl.BlockSpec(memory_space=pl.ANY)
     return pl.pallas_call(

time: 70 us -> 61.6 us (0.88)
  Pallas kernels: 65.3 us -> 57.6 us
    pallas_call x1, Pallas kernels: 65.3 us -> 57.6 us  [body(): pl.pallas_call(kernel, out_shape=(jax.ShapeDtypeStruct((TOK, BLK), BF16),...]
where the time goes in v6:
time: 61.6 us; the launch traced here: 61.4 us
  Pallas kernels  57.6 us (94%)
  local copies, waits for them, and re-layouts  3.14 us (5%)
  between operations  0.64 us (1%)
    pallas_call x1, Pallas kernels, body(): pl.pallas_call(kernel, out_shape=(jax.ShapeDtypeStruct((TOK, BLK), BF16),...  57.6 us
    unnamed x2, local copies, waits for them, and re-layouts  3.14 us

profile of v6, /device:TPU:6, one launch (start us, length us, event | category | flops | bytes accessed | tf_op | source)
XLA Modules:
  0.0 61.4 jit_solution(221158654535957381)
XLA Ops:
  0.6 57.6 %shard_map.95 = (bf16[256,512]{1,0:T(8,128)(2,1)}, bf16[256,128]{1,0:T(8,128)(2,1)}) custom-call(bf16[256,512]{1,0:T(8,128)(2,1)} %attn.1, s32[64]{0:T(128)} %signs.1, bf16[512,8192]{1,0:T(8,128)(2,1)} %w_out.1, s32[1,512]{1,0:T(1,128)} %bitcast.2, bf16[256,512]{1,0:T(8,128)(2,1)} %residual.1, bf16[512]{0:T(512)(128)(2,1)} %gain.1, bf16[8192,128]{1,0:T(8,128)(2,1)} %w_kv.1, ...), custom_call_target="tpu_custom_call" | custom-call | tf_op jit(solution)/shard_map/pallas_call | solution.py:438
  58.3 1.7 %copy.12 = bf16[256,512]{1,0:T(8,128)(2,1)} copy(bf16[256,512]{1,0:T(8,128)(2,1)} %get-tuple-element.4) | data formatting | bytes 524288
  59.9 1.5 %copy.13 = bf16[256,128]{1,0:T(8,128)(2,1)} copy(bf16[256,128]{1,0:T(8,128)(2,1)} %get-tuple-element.5) | data formatting | bytes 131072

commit v7 on v6

--- a/solution.py
+++ b/solution.py
@@ -18,7 +18,7 @@
 HALF = TOK // 2
 HCOL = BLK // 2
 LANES = 128
-PLANES = 4
+PLANES = 2
 SHARES = 2 * PLANES
 CK = BLK // SHARES
 PEERS = (
@@ -76,17 +76,11 @@
         return {"dp": lax.rem(z + k + nz, nz) * 2 + core}
 
     top = nz - 1
-    z_peers = (
-        (z < top, 1), (z > 0, -1), (z < top - 1, 2), (z > 1, -2),
-        ((z == 0) | (z == top - 3), 3), ((z == 3) | (z == top), -3),
+    z_peers = ((z < top, 1), (z > 0, -1))
+    z_sends = (
+        (z < top, 1, 0, CK // 2), (z > 0, -1, CK // 2, CK // 2),
+        (z == top - 1, 1, CK // 2, CK // 2), (z == 1, -1, 0, CK // 2),
     )
-    z_sends = (
-        (z < top, 1, 0, CK), (z > 0, -1, 0, CK),
-        (z < top - 1, 2, 0, CK // 2), ((z < top - 1) & (z >= top - 3), 2, CK // 2, CK // 2),
-        (z > 1, -2, CK // 2, CK // 2), ((z > 1) & (z <= 3), -2, 0, CK // 2),
-        (z == top - 3, 3, 0, CK), (z == 3, -3, 0, CK),
-    )
-
     sibling = {"dp": z * 2 + 1 - core}
 
     def send(src, dst, send_sem, recv_sem, to):
@@ -139,6 +133,8 @@
         columns = pl.ds(pl.multiple_of(at_yx(dy, dx) * BLK, BLK), BLK)
         w_loads[dy, dx] = pltpu.make_async_copy(w_out.at[:, columns], w.at[dy, dx], w_sem.at[i])
 
+    for dy, dx in ORDER:
+        w_loads[dy, dx].start()
     pl.semaphore_wait(barrier, N + sum(there.astype(jnp.int32) for there, _ in z_peers))
 
     def send_tokens(j):
@@ -147,13 +143,13 @@
 
     to_peers(send_tokens)
 
-    def send_kv_rows(j):
-        rows = pl.ds(pl.multiple_of(j * BLK + share * CK, CK), CK)
-        send(w_kv.at[rows, :], wkv.at[my_rows, my_cols], k_send, k_recv, {"tensor": j})
-
-    to_peers(send_kv_rows)
-    for dy, dx in ORDER:
-        w_loads[dy, dx].start()
+    def send_kv_rows(j, part):
+        low = part * (CK // 2)
+        rows = pl.ds(pl.multiple_of(j * BLK + share * CK + low, CK // 2), CK // 2)
+        slot = pl.ds(pl.multiple_of(share * CK + low, CK // 2), CK // 2)
+        send(w_kv.at[rows, :], wkv.at[slot, my_cols], k_send, k_recv, {"tensor": j})
+
+    to_peers(lambda j: send_kv_rows(j, 0))
 
     loads[0].wait()
     loads[1].wait()
@@ -174,6 +170,7 @@
         send(turned.at[j], rot.at[mine, :], r_send, r_recv, {"tensor": j})
 
     to_peers(send_turned)
+    to_peers(lambda j: send_kv_rows(j, 1))
     rot[mine, :] = turned[me]
 
     def z_start():
@@ -328,7 +325,6 @@
         ko[rows, :] = (total * scale).astype(BF16)
         pltpu.make_async_copy(ko.at[rows, :], kv_out.at[rows, :], out_sem.at[2 + half]).start()
 
-    z_start()
     wait(rot.at[pl.ds(0, (N - 1) * 16), :], r_recv)
 
     for i, (dy, dx) in enumerate(ORDER):
@@ -337,7 +333,9 @@
             first_far(0, dy)
         if dy == 2:
             first_far(1, dx)
-        for c in {6: (2,), 10: (1, 3), 14: (0,)}.get(i, ()):
+        if i == 6:
+            z_start()
+        for c in {6: (2,), 10: (1, 3)}.get(i, ()):
             first_near(0, c)
             first_near(1, c)
     for i in range(3, 7):
@@ -345,7 +343,10 @@
     for c in CHUNKS:
         second(0, c)
         second(1, c)
-        if c == 1:
+        if c == 2:
+            first_near(0, 0)
+            first_near(1, 0)
+        if c == 3:
             z_finish()
     squares = [residual_rows(0), residual_rows(1)]
     send_squares(*squares)

time: 61.6 us -> 59.3 us (0.963)
  Pallas kernels: 57.6 us -> 55.3 us
    pallas_call x1, Pallas kernels: 57.6 us -> 55.3 us  [body(): pl.pallas_call(kernel, out_shape=(jax.ShapeDtypeStruct((TOK, BLK), BF16),...]
where the time goes in v7:
time: 59.3 us; the launch traced here: 59.1 us
  Pallas kernels  55.3 us (93%)
  local copies, waits for them, and re-layouts  3.14 us (5%)
  between operations  0.64 us (1%)
    pallas_call x1, Pallas kernels, body(): pl.pallas_call(kernel, out_shape=(jax.ShapeDtypeStruct((TOK, BLK), BF16),...  55.3 us
    unnamed x2, local copies, waits for them, and re-layouts  3.14 us

profile of v7, /device:TPU:6, one launch (start us, length us, event | category | flops | bytes accessed | tf_op | source)
XLA Modules:
  0.0 59.1 jit_solution(13214643378606990661)
XLA Ops:
  0.6 55.3 %shard_map.95 = (bf16[256,512]{1,0:T(8,128)(2,1)}, bf16[256,128]{1,0:T(8,128)(2,1)}) custom-call(bf16[256,512]{1,0:T(8,128)(2,1)} %attn.1, s32[64]{0:T(128)} %signs.1, bf16[512,8192]{1,0:T(8,128)(2,1)} %w_out.1, s32[1,512]{1,0:T(1,128)} %bitcast.2, bf16[256,512]{1,0:T(8,128)(2,1)} %residual.1, bf16[512]{0:T(512)(128)(2,1)} %gain.1, bf16[8192,128]{1,0:T(8,128)(2,1)} %w_kv.1, ...), custom_call_target="tpu_custom_call" | custom-call | tf_op jit(solution)/shard_map/pallas_call | solution.py:439
  55.9 1.7 %copy.12 = bf16[256,512]{1,0:T(8,128)(2,1)} copy(bf16[256,512]{1,0:T(8,128)(2,1)} %get-tuple-element.4) | data formatting | bytes 524288
  57.6 1.5 %copy.13 = bf16[256,128]{1,0:T(8,128)(2,1)} copy(bf16[256,128]{1,0:T(8,128)(2,1)} %get-tuple-element.5) | data formatting | bytes 131072

commit v8 on v7

--- a/solution.py
+++ b/solution.py
@@ -17,6 +17,8 @@
 KVB = 128
 HALF = TOK // 2
 HCOL = BLK // 2
+PARTS = 2
+PROW = HALF // PARTS
 LANES = 128
 PLANES = 2
 SHARES = 2 * PLANES
@@ -48,7 +50,7 @@
 def kernel(
     attn, signs, w_out, out_exp, residual, gain, w_kv, kv_exp,
     resid_out, kv_out,
-    sgn, att, mixed, turned, rot, w, pb, s1, f, q, own, s1b, fb,
+    sgn, lane_signs, att, mixed, turned, rot, w, pb, s1, f, q, s1b, fb,
     wkv, xn, res, ro, gn, oe, ke, ko, sqs, sqr,
     pk, kf, kq, kown, kfb,
     in_sem, w_sem, out_sem,
@@ -151,14 +153,18 @@
 
     to_peers(lambda j: send_kv_rows(j, 0))
 
+    loads[1].wait()
+    for s in range(N):
+        for h in range(LH):
+            sign = (2 * sgn[s * LH + h] - 1).astype(F32)
+            lane_signs[s : s + 1, h * HD : (h + 1) * HD] = jnp.full((1, HD), sign)
     loads[0].wait()
-    loads[1].wait()
     wait(att.at[pl.ds(0, N - 1)], a_recv)
     for s in range(N):
         heads = []
         for h in range(LH):
-            sign = (2 * sgn[s * LH + h] - 1).astype(F32)
-            heads.append(att[s, :, h * HD : (h + 1) * HD].astype(F32) * sign)
+            at = slice(h * HD, (h + 1) * HD)
+            heads.append(att[s, :, at].astype(F32) * lane_signs[s : s + 1, at])
         for h, val in enumerate(hadamard(heads)):
             mixed[s, :, h * HD : (h + 1) * HD] = val
     for h in range(LH):
@@ -215,44 +221,50 @@
             pb[dy, dx, rows, part] = (
                 pb[dy, dx, rows, part].astype(F32) + s1[half, c, way].astype(F32)
             ).astype(BF16)
-            send(
-                pb.at[dy, dx, rows, :], f.at[half, c, way],
-                p_send, f_recv.at[half, c, way], along[half][way],
-            )
-
-    def second(half, c):
+            for p in range(PARTS):
+                send(
+                    pb.at[dy, dx, pl.ds(half * HALF + p * PROW, PROW), :],
+                    f.at[half, c, way, pl.ds(p * PROW, PROW), :],
+                    p_send, f_recv.at[half, c, way, p], along[half][way],
+                )
+
+    def first_total(half, c, p):
         dy, dx = block(half, c, 0)
-        total = pb[dy, dx, rows_of(half), :].astype(F32)
+        slot = pl.ds(p * PROW, PROW)
+        total = pb[dy, dx, pl.ds(half * HALF + p * PROW, PROW), :].astype(F32)
         for way in range(2):
-            wait(f.at[half, c, way], f_recv.at[half, c, way])
-            total = total + f[half, c, way].astype(F32)
-        if c == 0:
-            own[half] = total
-            return
+            wait(f.at[half, c, way, slot, :], f_recv.at[half, c, way, p])
+            total = total + f[half, c, way, slot, :].astype(F32)
+        return total
+
+    def second(half, c, p):
+        total = first_total(half, c, p)
+        slot = pl.ds(p * PROW, PROW)
         if c == 2:
-            q[half, 1] = total.astype(BF16)
+            q[half, 1, slot, :] = total.astype(BF16)
             for way in range(2):
                 send(
-                    q.at[half, 1, :, pl.ds(way * HCOL, HCOL)], s1b.at[half, way],
-                    q_send, s1b_recv.at[half, way], along[1 - half][way],
+                    q.at[half, 1, slot, pl.ds(way * HCOL, HCOL)], s1b.at[half, way, slot, :],
+                    q_send, s1b_recv.at[half, way, p], along[1 - half][way],
                 )
             return
         way = 0 if c == 1 else 1
         part = slice(way * HCOL, (way + 1) * HCOL)
         rest = slice((1 - way) * HCOL, (2 - way) * HCOL)
-        q[half, c - 1, :, rest] = total[:, rest].astype(BF16)
-        wait(s1b.at[half, way], s1b_recv.at[half, way])
-        q[half, c - 1, :, part] = (total[:, part] + s1b[half, way].astype(F32)).astype(BF16)
+        q[half, c - 1, slot, rest] = total[:, rest].astype(BF16)
+        wait(s1b.at[half, way, slot, :], s1b_recv.at[half, way, p])
+        q[half, c - 1, slot, part] = (total[:, part] + s1b[half, way, slot, :].astype(F32)).astype(BF16)
         send(
-            q.at[half, c - 1], fb.at[half, way],
-            q_send, fb_recv.at[half, way], along[1 - half][way],
+            q.at[half, c - 1, slot, :], fb.at[half, way, slot, :],
+            q_send, fb_recv.at[half, way, p], along[1 - half][way],
         )
 
     def residual_rows(half):
         rows = rows_of(half)
-        total = own[half]
+        total = jnp.concatenate([first_total(half, 0, p) for p in range(PARTS)], axis=0)
         for way in range(2):
-            wait(fb.at[half, way], fb_recv.at[half, way])
+            for p in range(PARTS):
+                wait(fb.at[half, way, pl.ds(p * PROW, PROW), :], fb_recv.at[half, way, p])
             total = total + fb[half, way].astype(F32)
         out = (res[rows, :].astype(F32) + total * jnp.exp2(oe[...].astype(F32))).astype(BF16)
         ro[rows, :] = out
@@ -279,14 +291,13 @@
         for k in range(4):
             pk[dy, lax.rem(k + 4 - x, 4)] = part[:, k * KVB : (k + 1) * KVB]
 
-    def kv_first(half, c):
-        for a in (2, 1, 3):
-            dy, dx = block(half, c, a)
-            to = at_yx(0, a) if half == 0 else at_yx(a, 0)
-            send(
-                pk.at[dy, dx, rows_of(half), :], kf.at[half, c, a - 1],
-                pk_send, kf_recv.at[half, c, a - 1], {"tensor": to},
-            )
+    def kv_first(half, c, a):
+        dy, dx = block(half, c, a)
+        to = at_yx(0, a) if half == 0 else at_yx(a, 0)
+        send(
+            pk.at[dy, dx, rows_of(half), :], kf.at[half, c, a - 1],
+            pk_send, kf_recv.at[half, c, a - 1], {"tensor": to},
+        )
 
     def kv_second(half, c):
         dy, dx = block(half, c, 0)
@@ -340,23 +351,25 @@
             first_near(1, c)
     for i in range(3, 7):
         loads[i].wait()
-    for c in CHUNKS:
-        second(0, c)
-        second(1, c)
+    for c in CHUNKS[:3]:
+        for p in range(PARTS):
+            second(0, c, p)
+            second(1, c, p)
         if c == 2:
             first_near(0, 0)
             first_near(1, 0)
         if c == 3:
             z_finish()
     squares = [residual_rows(0), residual_rows(1)]
+    wait(wkv.at[pl.ds(0, BLK // 2), :], sib_recv)
+    for d in CHUNKS:
+        product(d)
+        for a in (2, 1, 3):
+            kv_first(0, d, a)
+        if d:
+            for c in CHUNKS:
+                kv_first(1, c, d)
     send_squares(*squares)
-    wait(wkv.at[pl.ds(0, BLK // 2), :], sib_recv)
-    for c in CHUNKS:
-        product(c)
-        kv_first(0, c)
-        if c == 3:
-            for k in CHUNKS:
-                kv_first(1, k)
     for c in CHUNKS:
         if c == 0:
             scales = row_scales()
@@ -391,6 +404,7 @@
     dma = pltpu.SemaphoreType.DMA
     scratch = [
         pltpu.SMEM((N * LH,), jnp.int32),
+        vmem((N, BLK), F32),
         vmem((N, 16, BLK), BF16),
         vmem((N, 16, BLK), F32),
         vmem((N, 16, BLK), BF16),
@@ -400,7 +414,6 @@
         vmem((2, 4, 2, HALF, HCOL), BF16),
         vmem((2, 4, 2, HALF, BLK), BF16),
         vmem((2, 3, HALF, BLK), BF16),
-        vmem((2, HALF, BLK), F32),
         vmem((2, 2, HALF, HCOL), BF16),
         vmem((2, 2, HALF, BLK), BF16),
         vmem((BLK, N * KVB), BF16),
@@ -424,10 +437,10 @@
         dma, dma, dma, dma, dma, dma,
         dma,
         dma((2, 4, 2)),
-        dma((2, 4, 2)),
+        dma((2, 4, 2, PARTS)),
         dma,
-        dma((2, 2)),
-        dma((2, 2)),
+        dma((2, 2, PARTS)),
+        dma((2, 2, PARTS)),
         dma, dma, dma, dma,
         dma, dma,
         dma,

time: 59.3 us -> 58.8 us (level)
  no operation moved by 1% of the time
where the time goes in v8:
time: 58.8 us; the launch traced here: 58.6 us
  Pallas kernels  54.8 us (93%)
  local copies, waits for them, and re-layouts  3.14 us (5%)
  between operations  0.64 us (1%)
    pallas_call x1, Pallas kernels, body(): pl.pallas_call(kernel, out_shape=(jax.ShapeDtypeStruct((TOK, BLK), BF16),...  54.8 us
    unnamed x2, local copies, waits for them, and re-layouts  3.14 us

profile of v8, /device:TPU:6, one launch (start us, length us, event | category | flops | bytes accessed | tf_op | source)
XLA Modules:
  0.0 58.6 jit_solution(8857751718186427552)
XLA Ops:
  0.6 54.8 %shard_map.95 = (bf16[256,512]{1,0:T(8,128)(2,1)}, bf16[256,128]{1,0:T(8,128)(2,1)}) custom-call(bf16[256,512]{1,0:T(8,128)(2,1)} %attn.1, s32[64]{0:T(128)} %signs.1, bf16[512,8192]{1,0:T(8,128)(2,1)} %w_out.1, s32[1,512]{1,0:T(1,128)} %bitcast.2, bf16[256,512]{1,0:T(8,128)(2,1)} %residual.1, bf16[512]{0:T(512)(128)(2,1)} %gain.1, bf16[8192,128]{1,0:T(8,128)(2,1)} %w_kv.1, ...), custom_call_target="tpu_custom_call" | custom-call | tf_op jit(solution)/shard_map/pallas_call | solution.py:452
  55.4 1.7 %copy.12 = bf16[256,512]{1,0:T(8,128)(2,1)} copy(bf16[256,512]{1,0:T(8,128)(2,1)} %get-tuple-element.4) | data formatting | bytes 524288
  57.1 1.5 %copy.13 = bf16[256,128]{1,0:T(8,128)(2,1)} copy(bf16[256,128]{1,0:T(8,128)(2,1)} %get-tuple-element.5) | data formatting | bytes 131072
